TPU v7x, 512 devices: a whole 4x8x8 slice. The times are simulated.
512 devices in a mesh: src: 8 (over x, y_lo), gx: 16 (over z, core), gy: 4 (over y_hi).
Axes of the slice: x: 4, y: 8 (y_hi: 4, y_lo: 2; y = y_hi * 2 + y_lo), z: 8, core: 2. Of those that a mesh axis runs over, the one named last changes fastest.
Arguments:
- warm_potential: float32 [32, 64, 128, 128], P('src', 'gx', 'gy'), may hold values from -3 to 3
- warm_adjoint: float32 [32, 64, 128, 128], P('src', 'gx', 'gy'), may hold values from -3 to 3
- conductivity: float32 [64, 128, 128], P('gx', 'gy', 'src'), may hold values from 0.2 to 5
- electrodes: int32 [32, 2], replicated, may hold values from 0 to 8191
- receivers: int32 [128, 2], replicated, may hold values from 0 to 8191
- observed: float32 [32, 128], replicated, may hold values from -6 to 6
- source_order: int32 [32], replicated, may hold values from 0 to 31, each once
Outputs:
- gradient: float32 [64, 128, 128], P('gx', 'gy', 'src')
Inputs may be any that keep to these rules, and one draw needn't show every extreme that they name: `electrodes`: entries number surface cells as x * 128 + y. `receivers`: entries number surface cells as x * 128 + y.
All inputs are finite; a program needn't handle non-finite values.
Results may differ from a plain program's by a relative error of at most 0.0003.
Values sent between devices are 32-bit elements; how exact they have to be, the bound alone decides.
A program may use at most 64 MiB of HBM per device.

v0:
```python
import jax
import jax.numpy as jnp
from jax import lax
from jax.sharding import PartitionSpec as P

SWEEPS = 6
lowest = 0.05
highest = 2.0
centre = (highest + lowest) / 2.0
half_span = (highest - lowest) / 2.0
bound_ratio = centre / half_span
strength = 4.0


def padded_2(block, sides, width):
    for axis, dim in sides:
        count = lax.axis_size(axis)
        forward = [(i, i + 1) for i in range(count - 1)]
        backward = [(target, source) for source, target in forward]
        low = lax.ppermute(
            lax.slice_in_dim(block, block.shape[dim] - width, None, axis=dim), axis, forward
        )
        high = lax.ppermute(lax.slice_in_dim(block, 0, width, axis=dim), axis, backward)
        block = jnp.concatenate([low, block, high], axis=dim)
    return block


def harmonic(left, right):
    return jnp.where(right > 0, 2.0 * left * right / (left + right), left)


def slope_of(left, right):
    total = left + right
    return jnp.where(right > 0, 2.0 * right * right / (total * total), 1.0)


def neighbours(field, padded):
    widths = [(0, 0)] * (field.ndim - 1) + [(1, 1)]
    deeper = jnp.pad(field, widths)
    return (
        padded[..., :-2, 1:-1, :],
        padded[..., 2:, 1:-1, :],
        padded[..., 1:-1, :-2, :],
        padded[..., 1:-1, 2:, :],
        deeper[..., :-2],
        deeper[..., 2:],
    )


def face_tables(sigma, padded):
    others = neighbours(sigma, padded)
    depth = lax.broadcasted_iota(jnp.int32, sigma.shape, 2)
    surface = depth == 0
    coeffs = [harmonic(sigma, other) for other in others]
    slopes = [slope_of(sigma, other) for other in others]
    coeffs[4] = jnp.where(surface, 0.0, coeffs[4])
    slopes[4] = jnp.where(surface, 0.0, slopes[4])
    return (coeffs, slopes)


def apply_operator(field, padded, coeffs):
    others = neighbours(field, padded)
    total = coeffs[0] * (field - others[0])
    for index in range(1, 6):
        total = total + coeffs[index] * (field - others[index])
    return total


def solve(rhs, start, coeffs, inverse, pad_fn):
    residual = rhs - apply_operator(start, pad_fn(start), coeffs)
    update = inverse * residual / centre
    iterate = start
    factor = 1.0 / bound_ratio
    for sweep in range(SWEEPS):
        iterate = iterate + update
        residual = residual - apply_operator(update, pad_fn(update), coeffs)
        following = 1.0 / (2.0 * bound_ratio - factor)
        update = following * factor * update + 2.0 * following / half_span * (inverse * residual)
        factor = following
    return iterate + update


def gradient_term(potential, adjoint, padded_potential, padded_adjoint, slopes):
    near_potential = neighbours(potential, padded_potential)
    near_adjoint = neighbours(adjoint, padded_adjoint)
    total = slopes[0] * (potential - near_potential[0]) * (adjoint - near_adjoint[0])
    for index in range(1, 6):
        total = total + slopes[index] * (potential - near_potential[index]) * (
            adjoint - near_adjoint[index]
        )
    return total


def pad_joint(field):
    return padded_2(field, (("gx", 1), ("gy", 2)), 1)


def reduce_groups(partial_value, depth):
    summed = lax.psum(partial_value, "src")
    return lax.dynamic_slice_in_dim(summed, lax.axis_index("src") * depth, depth, 2)


def body(warm_potential, warm_adjoint, conductivity, electrodes, receivers, observed, source_order):
    panel = lax.all_gather(conductivity, "src", axis=2, tiled=True)
    group = lax.axis_index("src")
    slots = warm_potential.shape[0]
    width_x = panel.shape[0]
    ny_global = panel.shape[1] * lax.axis_size("gy")
    x_start = lax.axis_index("gx") * width_x
    potential_start, adjoint_start = (warm_potential, warm_adjoint)
    first_slot = group * slots
    y_start = lax.axis_index("gy") * panel.shape[1]
    width_y = panel.shape[1]
    depth_cells = panel.shape[2]
    coeffs, slopes = face_tables(panel, pad_joint(panel[None])[0])
    inverse = 1.0 / (coeffs[0] + coeffs[1] + coeffs[2] + coeffs[3] + coeffs[4] + coeffs[5])
    idents = lax.dynamic_slice_in_dim(source_order, first_slot, slots)
    pairs = jnp.take(electrodes, idents, axis=0)
    rows_observed = jnp.take(observed, idents, axis=0)

    def picker(cells):
        local_x = cells // ny_global - x_start
        local_y = cells % ny_global - y_start
        inside = (local_x >= 0) & (local_x < width_x) & (local_y >= 0) & (local_y < width_y)
        flat = local_x * width_y + local_y
        places = lax.broadcasted_iota(jnp.int32, (cells.shape[0], width_x * width_y), 1)
        return jnp.where((flat[:, None] == places) & inside[:, None], 1.0, 0.0).astype(jnp.float32)

    def on_surface(flat):
        field = jnp.zeros((slots, width_x, width_y, depth_cells), jnp.float32)
        return field.at[..., 0].set(flat.reshape(slots, width_x, width_y))

    source_surface = strength * (picker(pairs[:, 0]) - picker(pairs[:, 1]))
    potential = solve(on_surface(source_surface), potential_start, coeffs, inverse, pad_joint)
    pickup = picker(receivers[:, 0]) - picker(receivers[:, 1])
    top = potential[..., 0].reshape(slots, width_x * width_y)
    local_values = jnp.dot(
        top, pickup.T, precision=lax.Precision.HIGHEST, preferred_element_type=jnp.float32
    )
    predicted = lax.psum(local_values, ("gx", "gy"))
    misfit = predicted - rows_observed
    back = jnp.dot(
        misfit, pickup, precision=lax.Precision.HIGHEST, preferred_element_type=jnp.float32
    )
    adjoint = solve(on_surface(back), adjoint_start, coeffs, inverse, pad_joint)
    padded_both = pad_joint(jnp.concatenate([potential, adjoint], 0))
    term = gradient_term(potential, adjoint, padded_both[:slots], padded_both[slots:], slopes)
    partial_value = -jnp.sum(term, axis=0)
    return reduce_groups(partial_value, conductivity.shape[2])


def solution(mesh):
    in_specs = (
        P("src", "gx", "gy", None),
        P("src", "gx", "gy", None),
        P("gx", "gy", "src"),
        P(),
        P(),
        P(),
        P(),
    )
    out_specs = P("gx", "gy", "src")
    return jax.shard_map(body, mesh=mesh, in_specs=in_specs, out_specs=out_specs, check_vma=False)
```

profile of v0, /device:TPU:16, one launch (start us, length us, event | category | flops | bytes accessed | tf_op | source)
XLA Modules:
  0.0 592.4 jit_solution(16727907163246744626)
XLA Ops:
  7.3 29.0 %all_gather.3 = f32[4,32,128]{1,0,2:T(4,128)S(1)} all-gather(f32[4,32,16]{1,0,2:T(4,128)S(1)} %copy.69), channel_id=1, replica_groups=mesh['src'=8,'gx'=16,'gy'=4] {'src'}, dimensions={2}, use_global_device_ids=true | all-gather | bytes 73728 | tf_op jit(solution)/shard_map/all_gather | solution.py:104
  37.8 3.0 collective-permute-start
  40.9 3.9 collective-permute-start.4
  50.0 5.4 collective-permute-start.3
  55.4 2.6 collective-permute-start.2
  58.0 21.9 %collective-permute-done.3 = f32[1,6,1,128]{2,1,3,0:T(8,128)S(1)} collective-permute-done((f32[1,6,1,128]{2,1,3,0:T(8,128)S(1)}, f32[1,6,1,128]{2,1,3,0:T(8,128)S(1)}, u32[]{:S(2)}, u32[]{:S(2)}) %collective-permute-start.3) | collective-permute-done | bytes 3104 | tf_op jit(solution)/shard_map/ppermute | solution.py:23
  82.3 2.3 collective-permute-start.7
  84.7 5.6 collective-permute-start.6
  90.3 2.0 add_divide_fusion
  96.5 3.0 collective-permute-start.8
  100.5 1.9 collective-permute-start.11
  102.4 6.0 %collective-permute-start.10 = (f32[4,6,1,128]{3,2,1,0:T(1,128)S(1)}, f32[4,6,1,128]{3,2,1,0:T(1,128)S(1)}, u32[]{:S(2)}, u32[]{:S(2)}) collective-permute-start(f32[4,6,1,128]{3,2,1,0:T(1,128)S(1)} %get-tuple-element.118), channel_id=1, source_target_pairs={{0,1},{1,2},{2,3},{4,5},{5,6},{6,7},{8,9},{9,10},{10,11},{12,13},{... | collective-permute-start | bytes 36872 | tf_op jit(solution)/shard_map/ppermute | solution.py:20
  111.4 5.8 collective-permute-start.12
  118.2 1.9 collective-permute-start.15
  120.1 6.0 %collective-permute-start.14 = (f32[4,6,1,128]{3,2,1,0:T(1,128)S(1)}, f32[4,6,1,128]{3,2,1,0:T(1,128)S(1)}, u32[]{:S(2)}, u32[]{:S(2)}) collective-permute-start(f32[4,6,1,128]{3,2,1,0:T(1,128)S(1)} %get-tuple-element.116), channel_id=1, source_target_pairs={{0,1},{1,2},{2,3},{4,5},{5,6},{6,7},{8,9},{9,10},{10,11},{12,13},{... | collective-permute-start | bytes 36872 | tf_op jit(solution)/shard_map/ppermute | solution.py:20
  129.3 5.9 collective-permute-start.16
  136.1 1.9 collective-permute-start.19
  138.0 6.0 %collective-permute-start.18 = (f32[4,6,1,128]{3,2,1,0:T(1,128)S(1)}, f32[4,6,1,128]{3,2,1,0:T(1,128)S(1)}, u32[]{:S(2)}, u32[]{:S(2)}) collective-permute-start(f32[4,6,1,128]{3,2,1,0:T(1,128)S(1)} %get-tuple-element.114), channel_id=1, source_target_pairs={{0,1},{1,2},{2,3},{4,5},{5,6},{6,7},{8,9},{9,10},{10,11},{12,13},{... | collective-permute-start | bytes 36872 | tf_op jit(solution)/shard_map/ppermute | solution.py:20
  144.7 5.5 collective-permute-start.32
  153.2 5.8 collective-permute-start.20
  162.4 6.0 %collective-permute-start.22 = (f32[4,6,1,128]{3,2,1,0:T(1,128)}, f32[4,6,1,128]{3,2,1,0:T(1,128)}, u32[]{:S(2)}, u32[]{:S(2)}) collective-permute-start(f32[4,6,1,128]{3,2,1,0:T(1,128)} %get-tuple-element.112), channel_id=1, source_target_pairs={{0,1},{1,2},{2,3},{4,5},{5,6},{6,7},{8,9},{9,10},{10,11},{12,13},{... | collective-permute-start | bytes 36872 | tf_op jit(solution)/shard_map/ppermute | solution.py:20
  172.6 4.1 collective-permute-start.24
  177.6 1.9 collective-permute-start.27
  179.5 6.0 %collective-permute-start.26 = (f32[4,6,1,128]{3,2,1,0:T(1,128)S(1)}, f32[4,6,1,128]{3,2,1,0:T(1,128)S(1)}, u32[]{:S(2)}, u32[]{:S(2)}) collective-permute-start(f32[4,6,1,128]{3,2,1,0:T(1,128)S(1)} %get-tuple-element.110), channel_id=1, source_target_pairs={{0,1},{1,2},{2,3},{4,5},{5,6},{6,7},{8,9},{9,10},{10,11},{12,13},{... | collective-permute-start | bytes 36872 | tf_op jit(solution)/shard_map/ppermute | solution.py:20
  188.6 5.2 collective-permute-start.28
  196.6 6.0 %collective-permute-start.30 = (f32[4,6,1,128]{3,2,1,0:T(1,128)S(1)}, f32[4,6,1,128]{3,2,1,0:T(1,128)S(1)}, u32[]{:S(2)}, u32[]{:S(2)}) collective-permute-start(f32[4,6,1,128]{3,2,1,0:T(1,128)S(1)} %get-tuple-element.108), channel_id=1, source_target_pairs={{0,1},{1,2},{2,3},{4,5},{5,6},{6,7},{8,9},{9,10},{10,11},{12,13},{... | collective-permute-start | bytes 36872 | tf_op jit(solution)/shard_map/ppermute | solution.py:20
  204.6 6.0 %collective-permute-start.34 = (f32[4,6,1,128]{3,2,1,0:T(1,128)S(1)}, f32[4,6,1,128]{3,2,1,0:T(1,128)S(1)}, u32[]{:S(2)}, u32[]{:S(2)}) collective-permute-start(f32[4,6,1,128]{3,2,1,0:T(1,128)S(1)} %get-tuple-element.106), channel_id=1, source_target_pairs={{0,1},{1,2},{2,3},{4,5},{5,6},{6,7},{8,9},{9,10},{10,11},{12,13},{... | collective-permute-start | bytes 36872 | tf_op jit(solution)/shard_map/ppermute | solution.py:20
  212.4 144.6 %psum.14 = f32[4,128]{1,0:T(4,128)S(1)} all-reduce(f32[4,128]{1,0:T(4,128)S(1)} %fusion.300), channel_id=1, replica_groups=mesh['src'=8,'gx'=16,'gy'=4] {'gx','gy'}, use_global_device_ids=true, to_apply=%region_0.1 | all-reduce | flops 512 | bytes 4096 | tf_op jit(solution)/shard_map/psum | solution.py:140
  359.9 3.0 collective-permute-start.36
  363.9 4.6 collective-permute-start.39
  368.5 3.3 collective-permute-start.38
  371.9 3.1 collective-permute-done.38
  376.6 3.0 collective-permute-start.40
  382.5 6.0 %collective-permute-start.42 = (f32[4,6,1,128]{3,2,1,0:T(1,128)S(1)}, f32[4,6,1,128]{3,2,1,0:T(1,128)S(1)}, u32[]{:S(2)}, u32[]{:S(2)}) collective-permute-start(f32[4,6,1,128]{3,2,1,0:T(1,128)S(1)} %get-tuple-element.102), channel_id=1, source_target_pairs={{0,1},{1,2},{2,3},{4,5},{5,6},{6,7},{8,9},{9,10},{10,11},{12,13},{... | collective-permute-start | bytes 36872 | tf_op jit(solution)/shard_map/ppermute | solution.py:20
  391.5 4.1 collective-permute-start.44
  396.6 1.9 collective-permute-start.47
  398.5 6.2 %collective-permute-start.46 = (f32[4,6,1,128]{3,2,1,0:T(1,128)S(1)}, f32[4,6,1,128]{3,2,1,0:T(1,128)S(1)}, u32[]{:S(2)}, u32[]{:S(2)}) collective-permute-start(f32[4,6,1,128]{3,2,1,0:T(1,128)S(1)} %get-tuple-element.100), channel_id=1, source_target_pairs={{0,1},{1,2},{2,3},{4,5},{5,6},{6,7},{8,9},{9,10},{10,11},{12,13},{... | collective-permute-start | bytes 36872 | tf_op jit(solution)/shard_map/ppermute | solution.py:20
  407.5 5.9 collective-permute-start.48
  414.3 1.9 collective-permute-start.51
  416.3 6.0 %collective-permute-start.50 = (f32[4,6,1,128]{3,2,1,0:T(1,128)S(1)}, f32[4,6,1,128]{3,2,1,0:T(1,128)S(1)}, u32[]{:S(2)}, u32[]{:S(2)}) collective-permute-start(f32[4,6,1,128]{3,2,1,0:T(1,128)S(1)} %get-tuple-element.98), channel_id=1, source_target_pairs={{0,1},{1,2},{2,3},{4,5},{5,6},{6,7},{8,9},{9,10},{10,11},{12,13},{... | collective-permute-start | bytes 36872 | tf_op jit(solution)/shard_map/ppermute | solution.py:20
  425.3 5.6 collective-permute-start.52
  433.7 6.0 %collective-permute-start.54 = (f32[4,6,1,128]{3,2,1,0:T(1,128)S(1)}, f32[4,6,1,128]{3,2,1,0:T(1,128)S(1)}, u32[]{:S(2)}, u32[]{:S(2)}) collective-permute-start(f32[4,6,1,128]{3,2,1,0:T(1,128)S(1)} %get-tuple-element.96), channel_id=1, source_target_pairs={{0,1},{1,2},{2,3},{4,5},{5,6},{6,7},{8,9},{9,10},{10,11},{12,13},{... | collective-permute-start | bytes 36872 | tf_op jit(solution)/shard_map/ppermute | solution.py:20
  442.8 5.6 collective-permute-start.56
  451.2 6.0 %collective-permute-start.58 = (f32[4,6,1,128]{3,2,1,0:T(1,128)S(1)}, f32[4,6,1,128]{3,2,1,0:T(1,128)S(1)}, u32[]{:S(2)}, u32[]{:S(2)}) collective-permute-start(f32[4,6,1,128]{3,2,1,0:T(1,128)S(1)} %get-tuple-element.94), channel_id=1, source_target_pairs={{0,1},{1,2},{2,3},{4,5},{5,6},{6,7},{8,9},{9,10},{10,11},{12,13},{... | collective-permute-start | bytes 36872 | tf_op jit(solution)/shard_map/ppermute | solution.py:20
  460.4 5.7 collective-permute-start.60
  467.2 2.1 collective-permute-start.63
  469.2 6.0 %collective-permute-start.62 = (f32[8,6,1,128]{3,2,1,0:T(1,128)S(1)}, f32[8,6,1,128]{3,2,1,0:T(1,128)S(1)}, u32[]{:S(2)}, u32[]{:S(2)}) collective-permute-start(f32[8,6,1,128]{3,2,1,0:T(1,128)S(1)} %get-tuple-element.82), channel_id=1, source_target_pairs={{0,1},{1,2},{2,3},{4,5},{5,6},{6,7},{8,9},{9,10},{10,11},{12,13},{... | collective-permute-start | bytes 73736 | tf_op jit(solution)/shard_map/ppermute | solution.py:20
  477.8 106.1 %all-reduce.21.cloned.1.call-done = f32[4,32,128]{2,1,0:T(8,128)} async-done(((f32[4,32,128]{2,1,0:T(8,128)}), f32[4,32,128]{2,1,0:T(8,128)}) %all-reduce.21.cloned.1.call-update) | async-done | bytes 65552 | tf_op jit(solution)/shard_map/psum | solution.py:99
  (219 shorter events, 79.5 us)
Async XLA Ops:
  6.5 577.4 %all-reduce.21.cloned.1.call-start = ((), (), s32[]{:S(2)}) async-start(), calls=%async_computation | async-start | bytes 131072 | tf_op jit(solution)/shard_map/psum | solution.py:99
  36.5 13.1 %collective-permute-start.1 = (f32[1,1,32,128]{2,1,3,0:T(1,128)S(1)}, f32[1,1,32,128]{2,1,3,0:T(1,128)S(1)}, u32[]{:S(2)}, u32[]{:S(2)}) collective-permute-start(f32[1,1,32,128]{2,1,3,0:T(1,128)S(1)} %get-tuple-element.153), channel_id=1, source_target_pairs={{4,0},{8,4},{12,8},{16,12},{20,16},{24,20},{28,24},{32,28},{36,32}... | collective-permute-start | bytes 49160 | tf_op jit(solution)/shard_map/ppermute | solution.py:23
  37.8 11.8 %collective-permute-start = (f32[1,1,32,128]{2,1,3,0:T(1,128)S(1)}, f32[1,1,32,128]{2,1,3,0:T(1,128)S(1)}, u32[]{:S(2)}, u32[]{:S(2)}) collective-permute-start(f32[1,1,32,128]{2,1,3,0:T(1,128)S(1)} %get-tuple-element.152), channel_id=1, source_target_pairs={{0,4},{4,8},{8,12},{12,16},{16,20},{20,24},{24,28},{28,32},{32,36}... | collective-permute-start | bytes 49160 | tf_op jit(solution)/shard_map/ppermute | solution.py:20
  40.9 41.4 %collective-permute-start.4 = (f32[4,1,32,128]{3,2,1,0:T(8,128)S(1)}, f32[4,1,32,128]{3,2,1,0:T(8,128)S(1)}, u32[]{:S(2)}, u32[]{:S(2)}) collective-permute-start(f32[4,1,32,128]{3,2,1,0:T(8,128)S(1)} %get-tuple-element.151), channel_id=1, source_target_pairs={{0,4},{4,8},{8,12},{12,16},{16,20},{20,24},{24,28},{28,32},{32,36}... | collective-permute-start | bytes 196616 | tf_op jit(solution)/shard_map/ppermute | solution.py:20
  44.8 37.5 %collective-permute-start.5 = (f32[4,1,32,128]{3,2,1,0:T(8,128)S(1)}, f32[4,1,32,128]{3,2,1,0:T(8,128)S(1)}, u32[]{:S(2)}, u32[]{:S(2)}) collective-permute-start(f32[4,1,32,128]{3,2,1,0:T(8,128)S(1)} %get-tuple-element.150), channel_id=1, source_target_pairs={{4,0},{8,4},{12,8},{16,12},{20,16},{24,20},{28,24},{32,28},{36,32}... | collective-permute-start | bytes 196616 | tf_op jit(solution)/shard_map/ppermute | solution.py:23
  50.0 29.9 %collective-permute-start.3 = (f32[1,6,1,128]{2,1,3,0:T(8,128)S(1)}, f32[1,6,1,128]{2,1,3,0:T(8,128)S(1)}, u32[]{:S(2)}, u32[]{:S(2)}) collective-permute-start(f32[1,6,1,128]{2,1,3,0:T(8,128)S(1)} %get-tuple-element.93), channel_id=1, source_target_pairs={{1,0},{2,1},{3,2},{5,4},{6,5},{7,6},{9,8},{10,9},{11,10},{13,12},{... | collective-permute-start | bytes 9224 | tf_op jit(solution)/shard_map/ppermute | solution.py:23
  55.4 24.5 %collective-permute-start.2 = (f32[1,6,1,128]{2,1,3,0:T(8,128)S(1)}, f32[1,6,1,128]{2,1,3,0:T(8,128)S(1)}, u32[]{:S(2)}, u32[]{:S(2)}) collective-permute-start(f32[1,6,1,128]{2,1,3,0:T(8,128)S(1)} %get-tuple-element.92), channel_id=1, source_target_pairs={{0,1},{1,2},{2,3},{4,5},{5,6},{6,7},{8,9},{9,10},{10,11},{12,13},{... | collective-permute-start | bytes 9224 | tf_op jit(solution)/shard_map/ppermute | solution.py:20
  82.3 11.8 %collective-permute-start.7 = (f32[4,6,1,128]{3,2,1,0:T(1,128)S(1)}, f32[4,6,1,128]{3,2,1,0:T(1,128)S(1)}, u32[]{:S(2)}, u32[]{:S(2)}) collective-permute-start(f32[4,6,1,128]{3,2,1,0:T(1,128)S(1)} %get-tuple-element.121), channel_id=1, source_target_pairs={{1,0},{2,1},{3,2},{5,4},{6,5},{7,6},{9,8},{10,9},{11,10},{13,12},{... | collective-permute-start | bytes 36872 | tf_op jit(solution)/shard_map/ppermute | solution.py:23
  84.7 9.4 %collective-permute-start.6 = (f32[4,6,1,128]{3,2,1,0:T(1,128)S(1)}, f32[4,6,1,128]{3,2,1,0:T(1,128)S(1)}, u32[]{:S(2)}, u32[]{:S(2)}) collective-permute-start(f32[4,6,1,128]{3,2,1,0:T(1,128)S(1)} %get-tuple-element.120), channel_id=1, source_target_pairs={{0,1},{1,2},{2,3},{4,5},{5,6},{6,7},{8,9},{9,10},{10,11},{12,13},{... | collective-permute-start | bytes 36872 | tf_op jit(solution)/shard_map/ppermute | solution.py:20
  100.5 8.0 %collective-permute-start.11 = (f32[4,6,1,128]{3,2,1,0:T(1,128)S(1)}, f32[4,6,1,128]{3,2,1,0:T(1,128)S(1)}, u32[]{:S(2)}, u32[]{:S(2)}) collective-permute-start(f32[4,6,1,128]{3,2,1,0:T(1,128)S(1)} %get-tuple-element.119), channel_id=1, source_target_pairs={{1,0},{2,1},{3,2},{5,4},{6,5},{7,6},{9,8},{10,9},{11,10},{13,12},{... | collective-permute-start | bytes 36872 | tf_op jit(solution)/shard_map/ppermute | solution.py:23
  102.4 7.4 %collective-permute-start.10 = (f32[4,6,1,128]{3,2,1,0:T(1,128)S(1)}, f32[4,6,1,128]{3,2,1,0:T(1,128)S(1)}, u32[]{:S(2)}, u32[]{:S(2)}) collective-permute-start(f32[4,6,1,128]{3,2,1,0:T(1,128)S(1)} %get-tuple-element.118), channel_id=1, source_target_pairs={{0,1},{1,2},{2,3},{4,5},{5,6},{6,7},{8,9},{9,10},{10,11},{12,13},{... | collective-permute-start | bytes 36872 | tf_op jit(solution)/shard_map/ppermute | solution.py:20
  110.1 7.1 %collective-permute-start.13 = (f32[4,1,32,128]{3,2,1,0:T(8,128)S(1)}, f32[4,1,32,128]{3,2,1,0:T(8,128)S(1)}, u32[]{:S(2)}, u32[]{:S(2)}) collective-permute-start(f32[4,1,32,128]{3,2,1,0:T(8,128)S(1)} %get-tuple-element.147), channel_id=1, source_target_pairs={{4,0},{8,4},{12,8},{16,12},{20,16},{24,20},{28,24},{32,28},{36,32}... | collective-permute-start | bytes 196616 | tf_op jit(solution)/shard_map/ppermute | solution.py:23
  118.2 8.0 %collective-permute-start.15 = (f32[4,6,1,128]{3,2,1,0:T(1,128)S(1)}, f32[4,6,1,128]{3,2,1,0:T(1,128)S(1)}, u32[]{:S(2)}, u32[]{:S(2)}) collective-permute-start(f32[4,6,1,128]{3,2,1,0:T(1,128)S(1)} %get-tuple-element.117), channel_id=1, source_target_pairs={{1,0},{2,1},{3,2},{5,4},{6,5},{7,6},{9,8},{10,9},{11,10},{13,12},{... | collective-permute-start | bytes 36872 | tf_op jit(solution)/shard_map/ppermute | solution.py:23
  120.1 7.4 %collective-permute-start.14 = (f32[4,6,1,128]{3,2,1,0:T(1,128)S(1)}, f32[4,6,1,128]{3,2,1,0:T(1,128)S(1)}, u32[]{:S(2)}, u32[]{:S(2)}) collective-permute-start(f32[4,6,1,128]{3,2,1,0:T(1,128)S(1)} %get-tuple-element.116), channel_id=1, source_target_pairs={{0,1},{1,2},{2,3},{4,5},{5,6},{6,7},{8,9},{9,10},{10,11},{12,13},{... | collective-permute-start | bytes 36872 | tf_op jit(solution)/shard_map/ppermute | solution.py:20
  127.8 7.3 %collective-permute-start.17 = (f32[4,1,32,128]{3,2,1,0:T(8,128)S(1)}, f32[4,1,32,128]{3,2,1,0:T(8,128)S(1)}, u32[]{:S(2)}, u32[]{:S(2)}) collective-permute-start(f32[4,1,32,128]{3,2,1,0:T(8,128)S(1)} %get-tuple-element.145), channel_id=1, source_target_pairs={{4,0},{8,4},{12,8},{16,12},{20,16},{24,20},{28,24},{32,28},{36,32}... | collective-permute-start | bytes 196616 | tf_op jit(solution)/shard_map/ppermute | solution.py:23
  129.3 6.8 %collective-permute-start.16 = (f32[4,1,32,128]{3,2,1,0:T(8,128)S(1)}, f32[4,1,32,128]{3,2,1,0:T(8,128)S(1)}, u32[]{:S(2)}, u32[]{:S(2)}) collective-permute-start(f32[4,1,32,128]{3,2,1,0:T(8,128)S(1)} %get-tuple-element.144), channel_id=1, source_target_pairs={{0,4},{4,8},{8,12},{12,16},{16,20},{20,24},{24,28},{28,32},{32,36}... | collective-permute-start | bytes 196616 | tf_op jit(solution)/shard_map/ppermute | solution.py:20
  136.1 15.5 %collective-permute-start.19 = (f32[4,6,1,128]{3,2,1,0:T(1,128)S(1)}, f32[4,6,1,128]{3,2,1,0:T(1,128)S(1)}, u32[]{:S(2)}, u32[]{:S(2)}) collective-permute-start(f32[4,6,1,128]{3,2,1,0:T(1,128)S(1)} %get-tuple-element.115), channel_id=1, source_target_pairs={{1,0},{2,1},{3,2},{5,4},{6,5},{7,6},{9,8},{10,9},{11,10},{13,12},{... | collective-permute-start | bytes 36872 | tf_op jit(solution)/shard_map/ppermute | solution.py:23
  138.0 13.6 %collective-permute-start.18 = (f32[4,6,1,128]{3,2,1,0:T(1,128)S(1)}, f32[4,6,1,128]{3,2,1,0:T(1,128)S(1)}, u32[]{:S(2)}, u32[]{:S(2)}) collective-permute-start(f32[4,6,1,128]{3,2,1,0:T(1,128)S(1)} %get-tuple-element.114), channel_id=1, source_target_pairs={{0,1},{1,2},{2,3},{4,5},{5,6},{6,7},{8,9},{9,10},{10,11},{12,13},{... | collective-permute-start | bytes 36872 | tf_op jit(solution)/shard_map/ppermute | solution.py:20
  144.7 32.0 %collective-permute-start.32 = (f32[4,1,32,128]{3,2,1,0:T(8,128)}, f32[4,1,32,128]{3,2,1,0:T(8,128)S(1)}, u32[]{:S(2)}, u32[]{:S(2)}) collective-permute-start(f32[4,1,32,128]{3,2,1,0:T(8,128)} %get-tuple-element.137), channel_id=1, source_target_pairs={{0,4},{4,8},{8,12},{12,16},{16,20},{20,24},{24,28},{28,32},{32,36}... | collective-permute-start | bytes 196616 | tf_op jit(solution)/shard_map/ppermute | solution.py:20
  150.2 43.6 %collective-permute-start.33 = (f32[4,1,32,128]{3,2,1,0:T(8,128)}, f32[4,1,32,128]{3,2,1,0:T(8,128)}, u32[]{:S(2)}, u32[]{:S(2)}) collective-permute-start(f32[4,1,32,128]{3,2,1,0:T(8,128)} %get-tuple-element.136), channel_id=1, source_target_pairs={{4,0},{8,4},{12,8},{16,12},{20,16},{24,20},{28,24},{32,28},{36,32}... | collective-permute-start | bytes 196616 | tf_op jit(solution)/shard_map/ppermute | solution.py:23
  151.9 7.7 %collective-permute-start.21 = (f32[4,1,32,128]{3,2,1,0:T(8,128)S(1)}, f32[4,1,32,128]{3,2,1,0:T(8,128)S(1)}, u32[]{:S(2)}, u32[]{:S(2)}) collective-permute-start(f32[4,1,32,128]{3,2,1,0:T(8,128)S(1)} %get-tuple-element.143), channel_id=1, source_target_pairs={{4,0},{8,4},{12,8},{16,12},{20,16},{24,20},{28,24},{32,28},{36,32}... | collective-permute-start | bytes 196616 | tf_op jit(solution)/shard_map/ppermute | solution.py:23
  160.5 9.8 %collective-permute-start.23 = (f32[4,6,1,128]{3,2,1,0:T(1,128)}, f32[4,6,1,128]{3,2,1,0:T(1,128)}, u32[]{:S(2)}, u32[]{:S(2)}) collective-permute-start(f32[4,6,1,128]{3,2,1,0:T(1,128)} %get-tuple-element.113), channel_id=1, source_target_pairs={{1,0},{2,1},{3,2},{5,4},{6,5},{7,6},{9,8},{10,9},{11,10},{13,12},{... | collective-permute-start | bytes 36872 | tf_op jit(solution)/shard_map/ppermute | solution.py:23
  162.4 7.8 %collective-permute-start.22 = (f32[4,6,1,128]{3,2,1,0:T(1,128)}, f32[4,6,1,128]{3,2,1,0:T(1,128)}, u32[]{:S(2)}, u32[]{:S(2)}) collective-permute-start(f32[4,6,1,128]{3,2,1,0:T(1,128)} %get-tuple-element.112), channel_id=1, source_target_pairs={{0,1},{1,2},{2,3},{4,5},{5,6},{6,7},{8,9},{9,10},{10,11},{12,13},{... | collective-permute-start | bytes 36872 | tf_op jit(solution)/shard_map/ppermute | solution.py:20
  177.6 8.0 %collective-permute-start.27 = (f32[4,6,1,128]{3,2,1,0:T(1,128)S(1)}, f32[4,6,1,128]{3,2,1,0:T(1,128)S(1)}, u32[]{:S(2)}, u32[]{:S(2)}) collective-permute-start(f32[4,6,1,128]{3,2,1,0:T(1,128)S(1)} %get-tuple-element.111), channel_id=1, source_target_pairs={{1,0},{2,1},{3,2},{5,4},{6,5},{7,6},{9,8},{10,9},{11,10},{13,12},{... | collective-permute-start | bytes 36872 | tf_op jit(solution)/shard_map/ppermute | solution.py:23
  179.5 7.4 %collective-permute-start.26 = (f32[4,6,1,128]{3,2,1,0:T(1,128)S(1)}, f32[4,6,1,128]{3,2,1,0:T(1,128)S(1)}, u32[]{:S(2)}, u32[]{:S(2)}) collective-permute-start(f32[4,6,1,128]{3,2,1,0:T(1,128)S(1)} %get-tuple-element.110), channel_id=1, source_target_pairs={{0,1},{1,2},{2,3},{4,5},{5,6},{6,7},{8,9},{9,10},{10,11},{12,13},{... | collective-permute-start | bytes 36872 | tf_op jit(solution)/shard_map/ppermute | solution.py:20
  187.3 7.4 %collective-permute-start.29 = (f32[4,1,32,128]{3,2,1,0:T(8,128)S(1)}, f32[4,1,32,128]{3,2,1,0:T(8,128)S(1)}, u32[]{:S(2)}, u32[]{:S(2)}) collective-permute-start(f32[4,1,32,128]{3,2,1,0:T(8,128)S(1)} %get-tuple-element.139), channel_id=1, source_target_pairs={{4,0},{8,4},{12,8},{16,12},{20,16},{24,20},{28,24},{32,28},{36,32}... | collective-permute-start | bytes 196616 | tf_op jit(solution)/shard_map/ppermute | solution.py:23
  194.7 16.0 %collective-permute-start.31 = (f32[4,6,1,128]{3,2,1,0:T(1,128)S(1)}, f32[4,6,1,128]{3,2,1,0:T(1,128)S(1)}, u32[]{:S(2)}, u32[]{:S(2)}) collective-permute-start(f32[4,6,1,128]{3,2,1,0:T(1,128)S(1)} %get-tuple-element.109), channel_id=1, source_target_pairs={{1,0},{2,1},{3,2},{5,4},{6,5},{7,6},{9,8},{10,9},{11,10},{13,12},{... | collective-permute-start | bytes 36872 | tf_op jit(solution)/shard_map/ppermute | solution.py:23
  196.6 14.0 %collective-permute-start.30 = (f32[4,6,1,128]{3,2,1,0:T(1,128)S(1)}, f32[4,6,1,128]{3,2,1,0:T(1,128)S(1)}, u32[]{:S(2)}, u32[]{:S(2)}) collective-permute-start(f32[4,6,1,128]{3,2,1,0:T(1,128)S(1)} %get-tuple-element.108), channel_id=1, source_target_pairs={{0,1},{1,2},{2,3},{4,5},{5,6},{6,7},{8,9},{9,10},{10,11},{12,13},{... | collective-permute-start | bytes 36872 | tf_op jit(solution)/shard_map/ppermute | solution.py:20
  202.7 154.8 %collective-permute-start.35 = (f32[4,6,1,128]{3,2,1,0:T(1,128)S(1)}, f32[4,6,1,128]{3,2,1,0:T(1,128)S(1)}, u32[]{:S(2)}, u32[]{:S(2)}) collective-permute-start(f32[4,6,1,128]{3,2,1,0:T(1,128)S(1)} %get-tuple-element.107), channel_id=1, source_target_pairs={{1,0},{2,1},{3,2},{5,4},{6,5},{7,6},{9,8},{10,9},{11,10},{13,12},{... | collective-permute-start | bytes 36872 | tf_op jit(solution)/shard_map/ppermute | solution.py:23
  204.6 152.9 %collective-permute-start.34 = (f32[4,6,1,128]{3,2,1,0:T(1,128)S(1)}, f32[4,6,1,128]{3,2,1,0:T(1,128)S(1)}, u32[]{:S(2)}, u32[]{:S(2)}) collective-permute-start(f32[4,6,1,128]{3,2,1,0:T(1,128)S(1)} %get-tuple-element.106), channel_id=1, source_target_pairs={{0,1},{1,2},{2,3},{4,5},{5,6},{6,7},{8,9},{9,10},{10,11},{12,13},{... | collective-permute-start | bytes 36872 | tf_op jit(solution)/shard_map/ppermute | solution.py:20
  363.9 8.0 %collective-permute-start.39 = (f32[4,6,1,128]{3,2,1,0:T(1,128)S(1)}, f32[4,6,1,128]{3,2,1,0:T(1,128)S(1)}, u32[]{:S(2)}, u32[]{:S(2)}) collective-permute-start(f32[4,6,1,128]{3,2,1,0:T(1,128)S(1)} %get-tuple-element.105), channel_id=1, source_target_pairs={{1,0},{2,1},{3,2},{5,4},{6,5},{7,6},{9,8},{10,9},{11,10},{13,12},{... | collective-permute-start | bytes 36872 | tf_op jit(solution)/shard_map/ppermute | solution.py:23
  380.6 8.0 %collective-permute-start.43 = (f32[4,6,1,128]{3,2,1,0:T(1,128)S(1)}, f32[4,6,1,128]{3,2,1,0:T(1,128)S(1)}, u32[]{:S(2)}, u32[]{:S(2)}) collective-permute-start(f32[4,6,1,128]{3,2,1,0:T(1,128)S(1)} %get-tuple-element.103), channel_id=1, source_target_pairs={{1,0},{2,1},{3,2},{5,4},{6,5},{7,6},{9,8},{10,9},{11,10},{13,12},{... | collective-permute-start | bytes 36872 | tf_op jit(solution)/shard_map/ppermute | solution.py:23
  382.5 7.4 %collective-permute-start.42 = (f32[4,6,1,128]{3,2,1,0:T(1,128)S(1)}, f32[4,6,1,128]{3,2,1,0:T(1,128)S(1)}, u32[]{:S(2)}, u32[]{:S(2)}) collective-permute-start(f32[4,6,1,128]{3,2,1,0:T(1,128)S(1)} %get-tuple-element.102), channel_id=1, source_target_pairs={{0,1},{1,2},{2,3},{4,5},{5,6},{6,7},{8,9},{9,10},{10,11},{12,13},{... | collective-permute-start | bytes 36872 | tf_op jit(solution)/shard_map/ppermute | solution.py:20
  396.6 8.2 %collective-permute-start.47 = (f32[4,6,1,128]{3,2,1,0:T(1,128)S(1)}, f32[4,6,1,128]{3,2,1,0:T(1,128)S(1)}, u32[]{:S(2)}, u32[]{:S(2)}) collective-permute-start(f32[4,6,1,128]{3,2,1,0:T(1,128)S(1)} %get-tuple-element.101), channel_id=1, source_target_pairs={{1,0},{2,1},{3,2},{5,4},{6,5},{7,6},{9,8},{10,9},{11,10},{13,12},{... | collective-permute-start | bytes 36872 | tf_op jit(solution)/shard_map/ppermute | solution.py:23
  398.5 7.4 %collective-permute-start.46 = (f32[4,6,1,128]{3,2,1,0:T(1,128)S(1)}, f32[4,6,1,128]{3,2,1,0:T(1,128)S(1)}, u32[]{:S(2)}, u32[]{:S(2)}) collective-permute-start(f32[4,6,1,128]{3,2,1,0:T(1,128)S(1)} %get-tuple-element.100), channel_id=1, source_target_pairs={{0,1},{1,2},{2,3},{4,5},{5,6},{6,7},{8,9},{9,10},{10,11},{12,13},{... | collective-permute-start | bytes 36872 | tf_op jit(solution)/shard_map/ppermute | solution.py:20
  406.2 7.2 %collective-permute-start.49 = (f32[4,1,32,128]{3,2,1,0:T(8,128)S(1)}, f32[4,1,32,128]{3,2,1,0:T(8,128)S(1)}, u32[]{:S(2)}, u32[]{:S(2)}) collective-permute-start(f32[4,1,32,128]{3,2,1,0:T(8,128)S(1)} %get-tuple-element.129), channel_id=1, source_target_pairs={{4,0},{8,4},{12,8},{16,12},{20,16},{24,20},{28,24},{32,28},{36,32}... | collective-permute-start | bytes 196616 | tf_op jit(solution)/shard_map/ppermute | solution.py:23
  407.5 6.8 %collective-permute-start.48 = (f32[4,1,32,128]{3,2,1,0:T(8,128)S(1)}, f32[4,1,32,128]{3,2,1,0:T(8,128)S(1)}, u32[]{:S(2)}, u32[]{:S(2)}) collective-permute-start(f32[4,1,32,128]{3,2,1,0:T(8,128)S(1)} %get-tuple-element.128), channel_id=1, source_target_pairs={{0,4},{4,8},{8,12},{12,16},{16,20},{20,24},{24,28},{28,32},{32,36}... | collective-permute-start | bytes 196616 | tf_op jit(solution)/shard_map/ppermute | solution.py:20
  414.3 8.0 %collective-permute-start.51 = (f32[4,6,1,128]{3,2,1,0:T(1,128)S(1)}, f32[4,6,1,128]{3,2,1,0:T(1,128)S(1)}, u32[]{:S(2)}, u32[]{:S(2)}) collective-permute-start(f32[4,6,1,128]{3,2,1,0:T(1,128)S(1)} %get-tuple-element.99), channel_id=1, source_target_pairs={{1,0},{2,1},{3,2},{5,4},{6,5},{7,6},{9,8},{10,9},{11,10},{13,12},{... | collective-permute-start | bytes 36872 | tf_op jit(solution)/shard_map/ppermute | solution.py:23
  416.3 7.4 %collective-permute-start.50 = (f32[4,6,1,128]{3,2,1,0:T(1,128)S(1)}, f32[4,6,1,128]{3,2,1,0:T(1,128)S(1)}, u32[]{:S(2)}, u32[]{:S(2)}) collective-permute-start(f32[4,6,1,128]{3,2,1,0:T(1,128)S(1)} %get-tuple-element.98), channel_id=1, source_target_pairs={{0,1},{1,2},{2,3},{4,5},{5,6},{6,7},{8,9},{9,10},{10,11},{12,13},{... | collective-permute-start | bytes 36872 | tf_op jit(solution)/shard_map/ppermute | solution.py:20
  424.0 6.9 %collective-permute-start.53 = (f32[4,1,32,128]{3,2,1,0:T(8,128)S(1)}, f32[4,1,32,128]{3,2,1,0:T(8,128)S(1)}, u32[]{:S(2)}, u32[]{:S(2)}) collective-permute-start(f32[4,1,32,128]{3,2,1,0:T(8,128)S(1)} %get-tuple-element.127), channel_id=1, source_target_pairs={{4,0},{8,4},{12,8},{16,12},{20,16},{24,20},{28,24},{32,28},{36,32}... | collective-permute-start | bytes 196616 | tf_op jit(solution)/shard_map/ppermute | solution.py:23
  431.8 8.0 %collective-permute-start.55 = (f32[4,6,1,128]{3,2,1,0:T(1,128)S(1)}, f32[4,6,1,128]{3,2,1,0:T(1,128)S(1)}, u32[]{:S(2)}, u32[]{:S(2)}) collective-permute-start(f32[4,6,1,128]{3,2,1,0:T(1,128)S(1)} %get-tuple-element.97), channel_id=1, source_target_pairs={{1,0},{2,1},{3,2},{5,4},{6,5},{7,6},{9,8},{10,9},{11,10},{13,12},{... | collective-permute-start | bytes 36872 | tf_op jit(solution)/shard_map/ppermute | solution.py:23
  433.7 7.4 %collective-permute-start.54 = (f32[4,6,1,128]{3,2,1,0:T(1,128)S(1)}, f32[4,6,1,128]{3,2,1,0:T(1,128)S(1)}, u32[]{:S(2)}, u32[]{:S(2)}) collective-permute-start(f32[4,6,1,128]{3,2,1,0:T(1,128)S(1)} %get-tuple-element.96), channel_id=1, source_target_pairs={{0,1},{1,2},{2,3},{4,5},{5,6},{6,7},{8,9},{9,10},{10,11},{12,13},{... | collective-permute-start | bytes 36872 | tf_op jit(solution)/shard_map/ppermute | solution.py:20
  441.5 6.9 %collective-permute-start.57 = (f32[4,1,32,128]{3,2,1,0:T(8,128)S(1)}, f32[4,1,32,128]{3,2,1,0:T(8,128)S(1)}, u32[]{:S(2)}, u32[]{:S(2)}) collective-permute-start(f32[4,1,32,128]{3,2,1,0:T(8,128)S(1)} %get-tuple-element.125), channel_id=1, source_target_pairs={{4,0},{8,4},{12,8},{16,12},{20,16},{24,20},{28,24},{32,28},{36,32}... | collective-permute-start | bytes 196616 | tf_op jit(solution)/shard_map/ppermute | solution.py:23
  449.3 8.0 %collective-permute-start.59 = (f32[4,6,1,128]{3,2,1,0:T(1,128)S(1)}, f32[4,6,1,128]{3,2,1,0:T(1,128)S(1)}, u32[]{:S(2)}, u32[]{:S(2)}) collective-permute-start(f32[4,6,1,128]{3,2,1,0:T(1,128)S(1)} %get-tuple-element.95), channel_id=1, source_target_pairs={{1,0},{2,1},{3,2},{5,4},{6,5},{7,6},{9,8},{10,9},{11,10},{13,12},{... | collective-permute-start | bytes 36872 | tf_op jit(solution)/shard_map/ppermute | solution.py:23
  451.2 7.4 %collective-permute-start.58 = (f32[4,6,1,128]{3,2,1,0:T(1,128)S(1)}, f32[4,6,1,128]{3,2,1,0:T(1,128)S(1)}, u32[]{:S(2)}, u32[]{:S(2)}) collective-permute-start(f32[4,6,1,128]{3,2,1,0:T(1,128)S(1)} %get-tuple-element.94), channel_id=1, source_target_pairs={{0,1},{1,2},{2,3},{4,5},{5,6},{6,7},{8,9},{9,10},{10,11},{12,13},{... | collective-permute-start | bytes 36872 | tf_op jit(solution)/shard_map/ppermute | solution.py:20
  459.1 7.1 %collective-permute-start.61 = (f32[8,1,32,128]{3,2,1,0:T(8,128)S(1)}, f32[8,1,32,128]{3,2,1,0:T(8,128)S(1)}, u32[]{:S(2)}, u32[]{:S(2)}) collective-permute-start(f32[8,1,32,128]{3,2,1,0:T(8,128)S(1)} %get-tuple-element.91), channel_id=1, source_target_pairs={{4,0},{8,4},{12,8},{16,12},{20,16},{24,20},{28,24},{32,28},{36,32}... | collective-permute-start | bytes 393224 | tf_op jit(solution)/shard_map/ppermute | solution.py:23
  467.2 8.8 %collective-permute-start.63 = (f32[8,6,1,128]{3,2,1,0:T(1,128)S(1)}, f32[8,6,1,128]{3,2,1,0:T(1,128)S(1)}, u32[]{:S(2)}, u32[]{:S(2)}) collective-permute-start(f32[8,6,1,128]{3,2,1,0:T(1,128)S(1)} %get-tuple-element.83), channel_id=1, source_target_pairs={{1,0},{2,1},{3,2},{5,4},{6,5},{7,6},{9,8},{10,9},{11,10},{13,12},{... | collective-permute-start | bytes 73736 | tf_op jit(solution)/shard_map/ppermute | solution.py:23
  469.2 7.5 %collective-permute-start.62 = (f32[8,6,1,128]{3,2,1,0:T(1,128)S(1)}, f32[8,6,1,128]{3,2,1,0:T(1,128)S(1)}, u32[]{:S(2)}, u32[]{:S(2)}) collective-permute-start(f32[8,6,1,128]{3,2,1,0:T(1,128)S(1)} %get-tuple-element.82), channel_id=1, source_target_pairs={{0,1},{1,2},{2,3},{4,5},{5,6},{6,7},{8,9},{9,10},{10,11},{12,13},{... | collective-permute-start | bytes 73736 | tf_op jit(solution)/shard_map/ppermute | solution.py:20
  (38 other events, 802.2 us)
Sparse Core Ops, SparseCore 0:
  477.9 105.9 all-reduce.20
where the time goes:
time: 595 us; the launch traced here: 592 us
  starting transfers between devices  224 us (38%)
  blocking collectives  174 us (29%)
  waiting for transfers between devices  153 us (26%)
  other arithmetic  15 us (3%)
  between operations  14.6 us (2%)
  local copies, waits for them, and re-layouts  12.1 us (2%)
    ppermute x32, starting transfers between devices, padded_2(): lax.ppermute(lax.slice_in_dim(block, block.shape[dim] - width, None, axis...  166 us
    psum x1, blocking collectives, body(): predicted = lax.psum(local_values, ('gx', 'gy'))  145 us
    psum x1, waiting for transfers between devices, reduce_groups(): summed = lax.psum(partial_value, 'src')  106 us
    ppermute x32, starting transfers between devices, padded_2(): lax.ppermute(lax.slice_in_dim(block, 0, width, axis=dim), axis, backward)  58.2 us
    all_gather x1, blocking collectives, body(): panel = lax.all_gather(conductivity, 'src', axis=2, tiled=True)  29 us
    ppermute x32, waiting for transfers between devices, padded_2(): lax.ppermute(lax.slice_in_dim(block, block.shape[dim] - width, None, axis...  24.7 us
    ppermute x32, waiting for transfers between devices, padded_2(): lax.ppermute(lax.slice_in_dim(block, 0, width, axis=dim), axis, backward)  22 us
  transfers between devices with their start and end apart: 65, of which 24 were waited for; matrix products, arithmetic and copies ran while one was open for 3% of the time, Pallas kernels for 0%

commit v1 on v0

--- a/solution.py
+++ b/solution.py
@@ -137,7 +137,7 @@
     local_values = jnp.dot(
         top, pickup.T, precision=lax.Precision.HIGHEST, preferred_element_type=jnp.float32
     )
-    predicted = lax.psum(local_values, ("gx", "gy"))
+    predicted = lax.psum(lax.psum(local_values, "gy"), "gx")
     misfit = predicted - rows_observed
     back = jnp.dot(
         misfit, pickup, precision=lax.Precision.HIGHEST, preferred_element_type=jnp.float32

time: 595 us -> 488 us (0.82)
  blocking collectives: 174 us -> 72.3 us
  waiting for transfers between devices: 153 us -> 146 us
    psum x1 -> x2, blocking collectives: 145 us -> 43.3 us  [body(): predicted = lax.psum(lax.psum(local_values, 'gy'), 'gx')]
    psum x1, waiting for transfers between devices: 106 us -> 99.9 us  [reduce_groups(): summed = lax.psum(partial_value, 'src')]
where the time goes in v1:
time: 488 us; the launch traced here: 486 us
  starting transfers between devices  225 us (46%)
  waiting for transfers between devices  146 us (30%)
  blocking collectives  72.3 us (15%)
  other arithmetic  15 us (3%)
  between operations  14.6 us (3%)
  local copies, waits for them, and re-layouts  12.1 us (2%)
    ppermute x32, starting transfers between devices, padded_2(): lax.ppermute(lax.slice_in_dim(block, block.shape[dim] - width, None, axis...  167 us
    psum x1, waiting for transfers between devices, reduce_groups(): summed = lax.psum(partial_value, 'src')  99.9 us
    ppermute x32, starting transfers between devices, padded_2(): lax.ppermute(lax.slice_in_dim(block, 0, width, axis=dim), axis, backward)  58 us
    psum x2, blocking collectives, body(): predicted = lax.psum(lax.psum(local_values, 'gy'), 'gx')  43.3 us
    all_gather x1, blocking collectives, body(): panel = lax.all_gather(conductivity, 'src', axis=2, tiled=True)  29 us
    ppermute x32, waiting for transfers between devices, padded_2(): lax.ppermute(lax.slice_in_dim(block, block.shape[dim] - width, None, axis...  24.5 us
    ppermute x32, waiting for transfers between devices, padded_2(): lax.ppermute(lax.slice_in_dim(block, 0, width, axis=dim), axis, backward)  22 us
  transfers between devices with their start and end apart: 65, of which 24 were waited for; matrix products, arithmetic and copies ran while one was open for 3% of the time, Pallas kernels for 0%

profile of v1, /device:TPU:16, one launch (start us, length us, event | category | flops | bytes accessed | tf_op | source)
XLA Modules:
  0.0 486.2 jit_solution(8355135717633112644)
XLA Ops:
  7.3 29.0 %all_gather.3 = f32[4,32,128]{1,0,2:T(4,128)S(1)} all-gather(f32[4,32,16]{1,0,2:T(4,128)S(1)} %copy.69), channel_id=1, replica_groups=mesh['src'=8,'gx'=16,'gy'=4] {'src'}, dimensions={2}, use_global_device_ids=true | all-gather | bytes 73728 | tf_op jit(solution)/shard_map/all_gather | solution.py:104
  37.8 3.0 collective-permute-start
  40.9 3.9 collective-permute-start.4
  50.0 5.4 %collective-permute-start.3 = (f32[1,6,1,128]{2,1,3,0:T(8,128)S(1)}, f32[1,6,1,128]{2,1,3,0:T(8,128)S(1)}, u32[]{:S(2)}, u32[]{:S(2)}) collective-permute-start(f32[1,6,1,128]{2,1,3,0:T(8,128)S(1)} %get-tuple-element.93), channel_id=1, source_target_pairs={{1,0},{2,1},{3,2},{5,4},{6,5},{7,6},{9,8},{10,9},{11,10},{13,12},{... | collective-permute-start | bytes 9224 | tf_op jit(solution)/shard_map/ppermute | solution.py:23
  55.4 2.6 collective-permute-start.2
  58.0 21.9 %collective-permute-done.3 = f32[1,6,1,128]{2,1,3,0:T(8,128)S(1)} collective-permute-done((f32[1,6,1,128]{2,1,3,0:T(8,128)S(1)}, f32[1,6,1,128]{2,1,3,0:T(8,128)S(1)}, u32[]{:S(2)}, u32[]{:S(2)}) %collective-permute-start.3) | collective-permute-done | bytes 3104 | tf_op jit(solution)/shard_map/ppermute | solution.py:23
  82.3 2.3 collective-permute-start.7
  84.7 5.6 %collective-permute-start.6 = (f32[4,6,1,128]{3,2,1,0:T(1,128)S(1)}, f32[4,6,1,128]{3,2,1,0:T(1,128)S(1)}, u32[]{:S(2)}, u32[]{:S(2)}) collective-permute-start(f32[4,6,1,128]{3,2,1,0:T(1,128)S(1)} %get-tuple-element.120), channel_id=1, source_target_pairs={{0,1},{1,2},{2,3},{4,5},{5,6},{6,7},{8,9},{9,10},{10,11},{12,13},{... | collective-permute-start | bytes 36872 | tf_op jit(solution)/shard_map/ppermute | solution.py:20
  90.3 2.0 add_divide_fusion
  96.5 3.0 collective-permute-start.8
  100.5 1.9 collective-permute-start.11
  102.4 6.0 %collective-permute-start.10 = (f32[4,6,1,128]{3,2,1,0:T(1,128)S(1)}, f32[4,6,1,128]{3,2,1,0:T(1,128)S(1)}, u32[]{:S(2)}, u32[]{:S(2)}) collective-permute-start(f32[4,6,1,128]{3,2,1,0:T(1,128)S(1)} %get-tuple-element.118), channel_id=1, source_target_pairs={{0,1},{1,2},{2,3},{4,5},{5,6},{6,7},{8,9},{9,10},{10,11},{12,13},{... | collective-permute-start | bytes 36872 | tf_op jit(solution)/shard_map/ppermute | solution.py:20
  111.4 5.8 %collective-permute-start.12 = (f32[4,1,32,128]{3,2,1,0:T(8,128)S(1)}, f32[4,1,32,128]{3,2,1,0:T(8,128)S(1)}, u32[]{:S(2)}, u32[]{:S(2)}) collective-permute-start(f32[4,1,32,128]{3,2,1,0:T(8,128)S(1)} %get-tuple-element.146), channel_id=1, source_target_pairs={{0,4},{4,8},{8,12},{12,16},{16,20},{20,24},{24,28},{28,32},{32,36}... | collective-permute-start | bytes 196616 | tf_op jit(solution)/shard_map/ppermute | solution.py:20
  118.2 1.9 collective-permute-start.15
  120.1 6.0 %collective-permute-start.14 = (f32[4,6,1,128]{3,2,1,0:T(1,128)S(1)}, f32[4,6,1,128]{3,2,1,0:T(1,128)S(1)}, u32[]{:S(2)}, u32[]{:S(2)}) collective-permute-start(f32[4,6,1,128]{3,2,1,0:T(1,128)S(1)} %get-tuple-element.116), channel_id=1, source_target_pairs={{0,1},{1,2},{2,3},{4,5},{5,6},{6,7},{8,9},{9,10},{10,11},{12,13},{... | collective-permute-start | bytes 36872 | tf_op jit(solution)/shard_map/ppermute | solution.py:20
  129.3 5.9 %collective-permute-start.16 = (f32[4,1,32,128]{3,2,1,0:T(8,128)S(1)}, f32[4,1,32,128]{3,2,1,0:T(8,128)S(1)}, u32[]{:S(2)}, u32[]{:S(2)}) collective-permute-start(f32[4,1,32,128]{3,2,1,0:T(8,128)S(1)} %get-tuple-element.144), channel_id=1, source_target_pairs={{0,4},{4,8},{8,12},{12,16},{16,20},{20,24},{24,28},{28,32},{32,36}... | collective-permute-start | bytes 196616 | tf_op jit(solution)/shard_map/ppermute | solution.py:20
  138.0 6.0 %collective-permute-start.18 = (f32[4,6,1,128]{3,2,1,0:T(1,128)S(1)}, f32[4,6,1,128]{3,2,1,0:T(1,128)S(1)}, u32[]{:S(2)}, u32[]{:S(2)}) collective-permute-start(f32[4,6,1,128]{3,2,1,0:T(1,128)S(1)} %get-tuple-element.114), channel_id=1, source_target_pairs={{0,1},{1,2},{2,3},{4,5},{5,6},{6,7},{8,9},{9,10},{10,11},{12,13},{... | collective-permute-start | bytes 36872 | tf_op jit(solution)/shard_map/ppermute | solution.py:20
  144.7 5.5 %collective-permute-start.32 = (f32[4,1,32,128]{3,2,1,0:T(8,128)}, f32[4,1,32,128]{3,2,1,0:T(8,128)S(1)}, u32[]{:S(2)}, u32[]{:S(2)}) collective-permute-start(f32[4,1,32,128]{3,2,1,0:T(8,128)} %get-tuple-element.137), channel_id=1, source_target_pairs={{0,4},{4,8},{8,12},{12,16},{16,20},{20,24},{24,28},{28,32},{32,36}... | collective-permute-start | bytes 196616 | tf_op jit(solution)/shard_map/ppermute | solution.py:20
  153.2 5.8 %collective-permute-start.20 = (f32[4,1,32,128]{3,2,1,0:T(8,128)S(1)}, f32[4,1,32,128]{3,2,1,0:T(8,128)S(1)}, u32[]{:S(2)}, u32[]{:S(2)}) collective-permute-start(f32[4,1,32,128]{3,2,1,0:T(8,128)S(1)} %get-tuple-element.142), channel_id=1, source_target_pairs={{0,4},{4,8},{8,12},{12,16},{16,20},{20,24},{24,28},{28,32},{32,36}... | collective-permute-start | bytes 196616 | tf_op jit(solution)/shard_map/ppermute | solution.py:20
  162.4 6.0 %collective-permute-start.22 = (f32[4,6,1,128]{3,2,1,0:T(1,128)}, f32[4,6,1,128]{3,2,1,0:T(1,128)}, u32[]{:S(2)}, u32[]{:S(2)}) collective-permute-start(f32[4,6,1,128]{3,2,1,0:T(1,128)} %get-tuple-element.112), channel_id=1, source_target_pairs={{0,1},{1,2},{2,3},{4,5},{5,6},{6,7},{8,9},{9,10},{10,11},{12,13},{... | collective-permute-start | bytes 36872 | tf_op jit(solution)/shard_map/ppermute | solution.py:20
  172.6 4.1 collective-permute-start.24
  179.6 6.0 %collective-permute-start.26 = (f32[4,6,1,128]{3,2,1,0:T(1,128)S(1)}, f32[4,6,1,128]{3,2,1,0:T(1,128)S(1)}, u32[]{:S(2)}, u32[]{:S(2)}) collective-permute-start(f32[4,6,1,128]{3,2,1,0:T(1,128)S(1)} %get-tuple-element.110), channel_id=1, source_target_pairs={{0,1},{1,2},{2,3},{4,5},{5,6},{6,7},{8,9},{9,10},{10,11},{12,13},{... | collective-permute-start | bytes 36872 | tf_op jit(solution)/shard_map/ppermute | solution.py:20
  188.6 5.2 %collective-permute-start.28 = (f32[4,1,32,128]{3,2,1,0:T(8,128)S(1)}, f32[4,1,32,128]{3,2,1,0:T(8,128)S(1)}, u32[]{:S(2)}, u32[]{:S(2)}) collective-permute-start(f32[4,1,32,128]{3,2,1,0:T(8,128)S(1)} %get-tuple-element.138), channel_id=1, source_target_pairs={{0,4},{4,8},{8,12},{12,16},{16,20},{20,24},{24,28},{28,32},{32,36}... | collective-permute-start | bytes 196616 | tf_op jit(solution)/shard_map/ppermute | solution.py:20
  196.6 6.0 %collective-permute-start.30 = (f32[4,6,1,128]{3,2,1,0:T(1,128)S(1)}, f32[4,6,1,128]{3,2,1,0:T(1,128)S(1)}, u32[]{:S(2)}, u32[]{:S(2)}) collective-permute-start(f32[4,6,1,128]{3,2,1,0:T(1,128)S(1)} %get-tuple-element.108), channel_id=1, source_target_pairs={{0,1},{1,2},{2,3},{4,5},{5,6},{6,7},{8,9},{9,10},{10,11},{12,13},{... | collective-permute-start | bytes 36872 | tf_op jit(solution)/shard_map/ppermute | solution.py:20
  204.6 6.0 %collective-permute-start.34 = (f32[4,6,1,128]{3,2,1,0:T(1,128)S(1)}, f32[4,6,1,128]{3,2,1,0:T(1,128)S(1)}, u32[]{:S(2)}, u32[]{:S(2)}) collective-permute-start(f32[4,6,1,128]{3,2,1,0:T(1,128)S(1)} %get-tuple-element.106), channel_id=1, source_target_pairs={{0,1},{1,2},{2,3},{4,5},{5,6},{6,7},{8,9},{9,10},{10,11},{12,13},{... | collective-permute-start | bytes 36872 | tf_op jit(solution)/shard_map/ppermute | solution.py:20
  212.4 9.1 %psum.21 = f32[4,128]{1,0:T(4,128)S(1)} all-reduce(f32[4,128]{1,0:T(4,128)S(1)} %fusion.300), channel_id=1, replica_groups=mesh['src'=8,'gx'=16,'gy'=4] {'gy'}, use_global_device_ids=true, to_apply=%region_0.1 | all-reduce | flops 512 | bytes 4096 | tf_op jit(solution)/shard_map/psum | solution.py:140
  221.5 34.1 %psum.22 = f32[4,128]{1,0:T(4,128)S(1)} all-reduce(f32[4,128]{1,0:T(4,128)S(1)} %psum.21), channel_id=1, replica_groups=mesh['src'=8,'gx'=16,'gy'=4] {'gx'}, use_global_device_ids=true, to_apply=%region_1.2 | all-reduce | flops 512 | bytes 4096 | tf_op jit(solution)/shard_map/psum | solution.py:140
  258.6 3.0 collective-permute-start.36
  262.5 4.3 collective-permute-start.39
  266.9 3.6 collective-permute-start.38
  270.5 2.9 collective-permute-done.38
  275.0 3.1 collective-permute-start.40
  279.0 1.9 collective-permute-start.43
  281.0 6.0 %collective-permute-start.42 = (f32[4,6,1,128]{3,2,1,0:T(1,128)S(1)}, f32[4,6,1,128]{3,2,1,0:T(1,128)S(1)}, u32[]{:S(2)}, u32[]{:S(2)}) collective-permute-start(f32[4,6,1,128]{3,2,1,0:T(1,128)S(1)} %get-tuple-element.102), channel_id=1, source_target_pairs={{0,1},{1,2},{2,3},{4,5},{5,6},{6,7},{8,9},{9,10},{10,11},{12,13},{... | collective-permute-start | bytes 36872 | tf_op jit(solution)/shard_map/ppermute | solution.py:20
  290.0 5.8 %collective-permute-start.44 = (f32[4,1,32,128]{3,2,1,0:T(8,128)S(1)}, f32[4,1,32,128]{3,2,1,0:T(8,128)S(1)}, u32[]{:S(2)}, u32[]{:S(2)}) collective-permute-start(f32[4,1,32,128]{3,2,1,0:T(8,128)S(1)} %get-tuple-element.130), channel_id=1, source_target_pairs={{0,4},{4,8},{8,12},{12,16},{16,20},{20,24},{24,28},{28,32},{32,36}... | collective-permute-start | bytes 196616 | tf_op jit(solution)/shard_map/ppermute | solution.py:20
  296.5 1.9 collective-permute-start.47
  298.5 6.0 %collective-permute-start.46 = (f32[4,6,1,128]{3,2,1,0:T(1,128)S(1)}, f32[4,6,1,128]{3,2,1,0:T(1,128)S(1)}, u32[]{:S(2)}, u32[]{:S(2)}) collective-permute-start(f32[4,6,1,128]{3,2,1,0:T(1,128)S(1)} %get-tuple-element.100), channel_id=1, source_target_pairs={{0,1},{1,2},{2,3},{4,5},{5,6},{6,7},{8,9},{9,10},{10,11},{12,13},{... | collective-permute-start | bytes 36872 | tf_op jit(solution)/shard_map/ppermute | solution.py:20
  307.5 5.9 %collective-permute-start.48 = (f32[4,1,32,128]{3,2,1,0:T(8,128)S(1)}, f32[4,1,32,128]{3,2,1,0:T(8,128)S(1)}, u32[]{:S(2)}, u32[]{:S(2)}) collective-permute-start(f32[4,1,32,128]{3,2,1,0:T(8,128)S(1)} %get-tuple-element.128), channel_id=1, source_target_pairs={{0,4},{4,8},{8,12},{12,16},{16,20},{20,24},{24,28},{28,32},{32,36}... | collective-permute-start | bytes 196616 | tf_op jit(solution)/shard_map/ppermute | solution.py:20
  314.3 1.9 collective-permute-start.51
  316.2 6.0 %collective-permute-start.50 = (f32[4,6,1,128]{3,2,1,0:T(1,128)S(1)}, f32[4,6,1,128]{3,2,1,0:T(1,128)S(1)}, u32[]{:S(2)}, u32[]{:S(2)}) collective-permute-start(f32[4,6,1,128]{3,2,1,0:T(1,128)S(1)} %get-tuple-element.98), channel_id=1, source_target_pairs={{0,1},{1,2},{2,3},{4,5},{5,6},{6,7},{8,9},{9,10},{10,11},{12,13},{... | collective-permute-start | bytes 36872 | tf_op jit(solution)/shard_map/ppermute | solution.py:20
  325.3 5.6 %collective-permute-start.52 = (f32[4,1,32,128]{3,2,1,0:T(8,128)S(1)}, f32[4,1,32,128]{3,2,1,0:T(8,128)S(1)}, u32[]{:S(2)}, u32[]{:S(2)}) collective-permute-start(f32[4,1,32,128]{3,2,1,0:T(8,128)S(1)} %get-tuple-element.126), channel_id=1, source_target_pairs={{0,4},{4,8},{8,12},{12,16},{16,20},{20,24},{24,28},{28,32},{32,36}... | collective-permute-start | bytes 196616 | tf_op jit(solution)/shard_map/ppermute | solution.py:20
  333.7 6.0 %collective-permute-start.54 = (f32[4,6,1,128]{3,2,1,0:T(1,128)S(1)}, f32[4,6,1,128]{3,2,1,0:T(1,128)S(1)}, u32[]{:S(2)}, u32[]{:S(2)}) collective-permute-start(f32[4,6,1,128]{3,2,1,0:T(1,128)S(1)} %get-tuple-element.96), channel_id=1, source_target_pairs={{0,1},{1,2},{2,3},{4,5},{5,6},{6,7},{8,9},{9,10},{10,11},{12,13},{... | collective-permute-start | bytes 36872 | tf_op jit(solution)/shard_map/ppermute | solution.py:20
  342.7 5.6 %collective-permute-start.56 = (f32[4,1,32,128]{3,2,1,0:T(8,128)S(1)}, f32[4,1,32,128]{3,2,1,0:T(8,128)S(1)}, u32[]{:S(2)}, u32[]{:S(2)}) collective-permute-start(f32[4,1,32,128]{3,2,1,0:T(8,128)S(1)} %get-tuple-element.124), channel_id=1, source_target_pairs={{0,4},{4,8},{8,12},{12,16},{16,20},{20,24},{24,28},{28,32},{32,36}... | collective-permute-start | bytes 196616 | tf_op jit(solution)/shard_map/ppermute | solution.py:20
  351.2 6.0 %collective-permute-start.58 = (f32[4,6,1,128]{3,2,1,0:T(1,128)S(1)}, f32[4,6,1,128]{3,2,1,0:T(1,128)S(1)}, u32[]{:S(2)}, u32[]{:S(2)}) collective-permute-start(f32[4,6,1,128]{3,2,1,0:T(1,128)S(1)} %get-tuple-element.94), channel_id=1, source_target_pairs={{0,1},{1,2},{2,3},{4,5},{5,6},{6,7},{8,9},{9,10},{10,11},{12,13},{... | collective-permute-start | bytes 36872 | tf_op jit(solution)/shard_map/ppermute | solution.py:20
  360.4 5.7 %collective-permute-start.60 = (f32[8,1,32,128]{3,2,1,0:T(8,128)S(1)}, f32[8,1,32,128]{3,2,1,0:T(8,128)S(1)}, u32[]{:S(2)}, u32[]{:S(2)}) collective-permute-start(f32[8,1,32,128]{3,2,1,0:T(8,128)S(1)} %get-tuple-element.90), channel_id=1, source_target_pairs={{0,4},{4,8},{8,12},{12,16},{16,20},{20,24},{24,28},{28,32},{32,36}... | collective-permute-start | bytes 393224 | tf_op jit(solution)/shard_map/ppermute | solution.py:20
  367.1 2.1 collective-permute-start.63
  369.2 6.0 %collective-permute-start.62 = (f32[8,6,1,128]{3,2,1,0:T(1,128)S(1)}, f32[8,6,1,128]{3,2,1,0:T(1,128)S(1)}, u32[]{:S(2)}, u32[]{:S(2)}) collective-permute-start(f32[8,6,1,128]{3,2,1,0:T(1,128)S(1)} %get-tuple-element.82), channel_id=1, source_target_pairs={{0,1},{1,2},{2,3},{4,5},{5,6},{6,7},{8,9},{9,10},{10,11},{12,13},{... | collective-permute-start | bytes 73736 | tf_op jit(solution)/shard_map/ppermute | solution.py:20
  377.8 99.9 %all-reduce.21.cloned.1.call-done = f32[4,32,128]{2,1,0:T(8,128)} async-done(((f32[4,32,128]{2,1,0:T(8,128)}), f32[4,32,128]{2,1,0:T(8,128)}) %all-reduce.21.cloned.1.call-update) | async-done | bytes 65552 | tf_op jit(solution)/shard_map/psum | solution.py:99
  (220 shorter events, 81.5 us)
Async XLA Ops:
  6.5 471.2 %all-reduce.21.cloned.1.call-start = ((), (), s32[]{:S(2)}) async-start(), calls=%async_computation | async-start | bytes 131072 | tf_op jit(solution)/shard_map/psum | solution.py:99
  36.5 13.1 %collective-permute-start.1 = (f32[1,1,32,128]{2,1,3,0:T(1,128)S(1)}, f32[1,1,32,128]{2,1,3,0:T(1,128)S(1)}, u32[]{:S(2)}, u32[]{:S(2)}) collective-permute-start(f32[1,1,32,128]{2,1,3,0:T(1,128)S(1)} %get-tuple-element.153), channel_id=1, source_target_pairs={{4,0},{8,4},{12,8},{16,12},{20,16},{24,20},{28,24},{32,28},{36,32}... | collective-permute-start | bytes 49160 | tf_op jit(solution)/shard_map/ppermute | solution.py:23
  37.8 11.8 %collective-permute-start = (f32[1,1,32,128]{2,1,3,0:T(1,128)S(1)}, f32[1,1,32,128]{2,1,3,0:T(1,128)S(1)}, u32[]{:S(2)}, u32[]{:S(2)}) collective-permute-start(f32[1,1,32,128]{2,1,3,0:T(1,128)S(1)} %get-tuple-element.152), channel_id=1, source_target_pairs={{0,4},{4,8},{8,12},{12,16},{16,20},{20,24},{24,28},{28,32},{32,36}... | collective-permute-start | bytes 49160 | tf_op jit(solution)/shard_map/ppermute | solution.py:20
  40.9 41.4 %collective-permute-start.4 = (f32[4,1,32,128]{3,2,1,0:T(8,128)S(1)}, f32[4,1,32,128]{3,2,1,0:T(8,128)S(1)}, u32[]{:S(2)}, u32[]{:S(2)}) collective-permute-start(f32[4,1,32,128]{3,2,1,0:T(8,128)S(1)} %get-tuple-element.151), channel_id=1, source_target_pairs={{0,4},{4,8},{8,12},{12,16},{16,20},{20,24},{24,28},{28,32},{32,36}... | collective-permute-start | bytes 196616 | tf_op jit(solution)/shard_map/ppermute | solution.py:20
  44.8 37.5 %collective-permute-start.5 = (f32[4,1,32,128]{3,2,1,0:T(8,128)S(1)}, f32[4,1,32,128]{3,2,1,0:T(8,128)S(1)}, u32[]{:S(2)}, u32[]{:S(2)}) collective-permute-start(f32[4,1,32,128]{3,2,1,0:T(8,128)S(1)} %get-tuple-element.150), channel_id=1, source_target_pairs={{4,0},{8,4},{12,8},{16,12},{20,16},{24,20},{28,24},{32,28},{36,32}... | collective-permute-start | bytes 196616 | tf_op jit(solution)/shard_map/ppermute | solution.py:23
  50.0 29.9 %collective-permute-start.3 = (f32[1,6,1,128]{2,1,3,0:T(8,128)S(1)}, f32[1,6,1,128]{2,1,3,0:T(8,128)S(1)}, u32[]{:S(2)}, u32[]{:S(2)}) collective-permute-start(f32[1,6,1,128]{2,1,3,0:T(8,128)S(1)} %get-tuple-element.93), channel_id=1, source_target_pairs={{1,0},{2,1},{3,2},{5,4},{6,5},{7,6},{9,8},{10,9},{11,10},{13,12},{... | collective-permute-start | bytes 9224 | tf_op jit(solution)/shard_map/ppermute | solution.py:23
  55.4 24.5 %collective-permute-start.2 = (f32[1,6,1,128]{2,1,3,0:T(8,128)S(1)}, f32[1,6,1,128]{2,1,3,0:T(8,128)S(1)}, u32[]{:S(2)}, u32[]{:S(2)}) collective-permute-start(f32[1,6,1,128]{2,1,3,0:T(8,128)S(1)} %get-tuple-element.92), channel_id=1, source_target_pairs={{0,1},{1,2},{2,3},{4,5},{5,6},{6,7},{8,9},{9,10},{10,11},{12,13},{... | collective-permute-start | bytes 9224 | tf_op jit(solution)/shard_map/ppermute | solution.py:20
  82.3 11.8 %collective-permute-start.7 = (f32[4,6,1,128]{3,2,1,0:T(1,128)S(1)}, f32[4,6,1,128]{3,2,1,0:T(1,128)S(1)}, u32[]{:S(2)}, u32[]{:S(2)}) collective-permute-start(f32[4,6,1,128]{3,2,1,0:T(1,128)S(1)} %get-tuple-element.121), channel_id=1, source_target_pairs={{1,0},{2,1},{3,2},{5,4},{6,5},{7,6},{9,8},{10,9},{11,10},{13,12},{... | collective-permute-start | bytes 36872 | tf_op jit(solution)/shard_map/ppermute | solution.py:23
  84.7 9.4 %collective-permute-start.6 = (f32[4,6,1,128]{3,2,1,0:T(1,128)S(1)}, f32[4,6,1,128]{3,2,1,0:T(1,128)S(1)}, u32[]{:S(2)}, u32[]{:S(2)}) collective-permute-start(f32[4,6,1,128]{3,2,1,0:T(1,128)S(1)} %get-tuple-element.120), channel_id=1, source_target_pairs={{0,1},{1,2},{2,3},{4,5},{5,6},{6,7},{8,9},{9,10},{10,11},{12,13},{... | collective-permute-start | bytes 36872 | tf_op jit(solution)/shard_map/ppermute | solution.py:20
  100.5 8.0 %collective-permute-start.11 = (f32[4,6,1,128]{3,2,1,0:T(1,128)S(1)}, f32[4,6,1,128]{3,2,1,0:T(1,128)S(1)}, u32[]{:S(2)}, u32[]{:S(2)}) collective-permute-start(f32[4,6,1,128]{3,2,1,0:T(1,128)S(1)} %get-tuple-element.119), channel_id=1, source_target_pairs={{1,0},{2,1},{3,2},{5,4},{6,5},{7,6},{9,8},{10,9},{11,10},{13,12},{... | collective-permute-start | bytes 36872 | tf_op jit(solution)/shard_map/ppermute | solution.py:23
  102.4 7.4 %collective-permute-start.10 = (f32[4,6,1,128]{3,2,1,0:T(1,128)S(1)}, f32[4,6,1,128]{3,2,1,0:T(1,128)S(1)}, u32[]{:S(2)}, u32[]{:S(2)}) collective-permute-start(f32[4,6,1,128]{3,2,1,0:T(1,128)S(1)} %get-tuple-element.118), channel_id=1, source_target_pairs={{0,1},{1,2},{2,3},{4,5},{5,6},{6,7},{8,9},{9,10},{10,11},{12,13},{... | collective-permute-start | bytes 36872 | tf_op jit(solution)/shard_map/ppermute | solution.py:20
  110.1 7.1 %collective-permute-start.13 = (f32[4,1,32,128]{3,2,1,0:T(8,128)S(1)}, f32[4,1,32,128]{3,2,1,0:T(8,128)S(1)}, u32[]{:S(2)}, u32[]{:S(2)}) collective-permute-start(f32[4,1,32,128]{3,2,1,0:T(8,128)S(1)} %get-tuple-element.147), channel_id=1, source_target_pairs={{4,0},{8,4},{12,8},{16,12},{20,16},{24,20},{28,24},{32,28},{36,32}... | collective-permute-start | bytes 196616 | tf_op jit(solution)/shard_map/ppermute | solution.py:23
  118.2 8.0 %collective-permute-start.15 = (f32[4,6,1,128]{3,2,1,0:T(1,128)S(1)}, f32[4,6,1,128]{3,2,1,0:T(1,128)S(1)}, u32[]{:S(2)}, u32[]{:S(2)}) collective-permute-start(f32[4,6,1,128]{3,2,1,0:T(1,128)S(1)} %get-tuple-element.117), channel_id=1, source_target_pairs={{1,0},{2,1},{3,2},{5,4},{6,5},{7,6},{9,8},{10,9},{11,10},{13,12},{... | collective-permute-start | bytes 36872 | tf_op jit(solution)/shard_map/ppermute | solution.py:23
  120.1 7.4 %collective-permute-start.14 = (f32[4,6,1,128]{3,2,1,0:T(1,128)S(1)}, f32[4,6,1,128]{3,2,1,0:T(1,128)S(1)}, u32[]{:S(2)}, u32[]{:S(2)}) collective-permute-start(f32[4,6,1,128]{3,2,1,0:T(1,128)S(1)} %get-tuple-element.116), channel_id=1, source_target_pairs={{0,1},{1,2},{2,3},{4,5},{5,6},{6,7},{8,9},{9,10},{10,11},{12,13},{... | collective-permute-start | bytes 36872 | tf_op jit(solution)/shard_map/ppermute | solution.py:20
  127.8 7.3 %collective-permute-start.17 = (f32[4,1,32,128]{3,2,1,0:T(8,128)S(1)}, f32[4,1,32,128]{3,2,1,0:T(8,128)S(1)}, u32[]{:S(2)}, u32[]{:S(2)}) collective-permute-start(f32[4,1,32,128]{3,2,1,0:T(8,128)S(1)} %get-tuple-element.145), channel_id=1, source_target_pairs={{4,0},{8,4},{12,8},{16,12},{20,16},{24,20},{28,24},{32,28},{36,32}... | collective-permute-start | bytes 196616 | tf_op jit(solution)/shard_map/ppermute | solution.py:23
  129.3 6.8 %collective-permute-start.16 = (f32[4,1,32,128]{3,2,1,0:T(8,128)S(1)}, f32[4,1,32,128]{3,2,1,0:T(8,128)S(1)}, u32[]{:S(2)}, u32[]{:S(2)}) collective-permute-start(f32[4,1,32,128]{3,2,1,0:T(8,128)S(1)} %get-tuple-element.144), channel_id=1, source_target_pairs={{0,4},{4,8},{8,12},{12,16},{16,20},{20,24},{24,28},{28,32},{32,36}... | collective-permute-start | bytes 196616 | tf_op jit(solution)/shard_map/ppermute | solution.py:20
  136.1 15.5 %collective-permute-start.19 = (f32[4,6,1,128]{3,2,1,0:T(1,128)S(1)}, f32[4,6,1,128]{3,2,1,0:T(1,128)S(1)}, u32[]{:S(2)}, u32[]{:S(2)}) collective-permute-start(f32[4,6,1,128]{3,2,1,0:T(1,128)S(1)} %get-tuple-element.115), channel_id=1, source_target_pairs={{1,0},{2,1},{3,2},{5,4},{6,5},{7,6},{9,8},{10,9},{11,10},{13,12},{... | collective-permute-start | bytes 36872 | tf_op jit(solution)/shard_map/ppermute | solution.py:23
  138.0 13.6 %collective-permute-start.18 = (f32[4,6,1,128]{3,2,1,0:T(1,128)S(1)}, f32[4,6,1,128]{3,2,1,0:T(1,128)S(1)}, u32[]{:S(2)}, u32[]{:S(2)}) collective-permute-start(f32[4,6,1,128]{3,2,1,0:T(1,128)S(1)} %get-tuple-element.114), channel_id=1, source_target_pairs={{0,1},{1,2},{2,3},{4,5},{5,6},{6,7},{8,9},{9,10},{10,11},{12,13},{... | collective-permute-start | bytes 36872 | tf_op jit(solution)/shard_map/ppermute | solution.py:20
  144.7 32.1 %collective-permute-start.32 = (f32[4,1,32,128]{3,2,1,0:T(8,128)}, f32[4,1,32,128]{3,2,1,0:T(8,128)S(1)}, u32[]{:S(2)}, u32[]{:S(2)}) collective-permute-start(f32[4,1,32,128]{3,2,1,0:T(8,128)} %get-tuple-element.137), channel_id=1, source_target_pairs={{0,4},{4,8},{8,12},{12,16},{16,20},{20,24},{24,28},{28,32},{32,36}... | collective-permute-start | bytes 196616 | tf_op jit(solution)/shard_map/ppermute | solution.py:20
  150.2 43.6 %collective-permute-start.33 = (f32[4,1,32,128]{3,2,1,0:T(8,128)}, f32[4,1,32,128]{3,2,1,0:T(8,128)}, u32[]{:S(2)}, u32[]{:S(2)}) collective-permute-start(f32[4,1,32,128]{3,2,1,0:T(8,128)} %get-tuple-element.136), channel_id=1, source_target_pairs={{4,0},{8,4},{12,8},{16,12},{20,16},{24,20},{28,24},{32,28},{36,32}... | collective-permute-start | bytes 196616 | tf_op jit(solution)/shard_map/ppermute | solution.py:23
  151.9 7.7 %collective-permute-start.21 = (f32[4,1,32,128]{3,2,1,0:T(8,128)S(1)}, f32[4,1,32,128]{3,2,1,0:T(8,128)S(1)}, u32[]{:S(2)}, u32[]{:S(2)}) collective-permute-start(f32[4,1,32,128]{3,2,1,0:T(8,128)S(1)} %get-tuple-element.143), channel_id=1, source_target_pairs={{4,0},{8,4},{12,8},{16,12},{20,16},{24,20},{28,24},{32,28},{36,32}... | collective-permute-start | bytes 196616 | tf_op jit(solution)/shard_map/ppermute | solution.py:23
  160.5 9.8 %collective-permute-start.23 = (f32[4,6,1,128]{3,2,1,0:T(1,128)}, f32[4,6,1,128]{3,2,1,0:T(1,128)}, u32[]{:S(2)}, u32[]{:S(2)}) collective-permute-start(f32[4,6,1,128]{3,2,1,0:T(1,128)} %get-tuple-element.113), channel_id=1, source_target_pairs={{1,0},{2,1},{3,2},{5,4},{6,5},{7,6},{9,8},{10,9},{11,10},{13,12},{... | collective-permute-start | bytes 36872 | tf_op jit(solution)/shard_map/ppermute | solution.py:23
  162.4 7.9 %collective-permute-start.22 = (f32[4,6,1,128]{3,2,1,0:T(1,128)}, f32[4,6,1,128]{3,2,1,0:T(1,128)}, u32[]{:S(2)}, u32[]{:S(2)}) collective-permute-start(f32[4,6,1,128]{3,2,1,0:T(1,128)} %get-tuple-element.112), channel_id=1, source_target_pairs={{0,1},{1,2},{2,3},{4,5},{5,6},{6,7},{8,9},{9,10},{10,11},{12,13},{... | collective-permute-start | bytes 36872 | tf_op jit(solution)/shard_map/ppermute | solution.py:20
  177.7 8.0 %collective-permute-start.27 = (f32[4,6,1,128]{3,2,1,0:T(1,128)S(1)}, f32[4,6,1,128]{3,2,1,0:T(1,128)S(1)}, u32[]{:S(2)}, u32[]{:S(2)}) collective-permute-start(f32[4,6,1,128]{3,2,1,0:T(1,128)S(1)} %get-tuple-element.111), channel_id=1, source_target_pairs={{1,0},{2,1},{3,2},{5,4},{6,5},{7,6},{9,8},{10,9},{11,10},{13,12},{... | collective-permute-start | bytes 36872 | tf_op jit(solution)/shard_map/ppermute | solution.py:23
  179.6 7.4 %collective-permute-start.26 = (f32[4,6,1,128]{3,2,1,0:T(1,128)S(1)}, f32[4,6,1,128]{3,2,1,0:T(1,128)S(1)}, u32[]{:S(2)}, u32[]{:S(2)}) collective-permute-start(f32[4,6,1,128]{3,2,1,0:T(1,128)S(1)} %get-tuple-element.110), channel_id=1, source_target_pairs={{0,1},{1,2},{2,3},{4,5},{5,6},{6,7},{8,9},{9,10},{10,11},{12,13},{... | collective-permute-start | bytes 36872 | tf_op jit(solution)/shard_map/ppermute | solution.py:20
  187.3 7.3 %collective-permute-start.29 = (f32[4,1,32,128]{3,2,1,0:T(8,128)S(1)}, f32[4,1,32,128]{3,2,1,0:T(8,128)S(1)}, u32[]{:S(2)}, u32[]{:S(2)}) collective-permute-start(f32[4,1,32,128]{3,2,1,0:T(8,128)S(1)} %get-tuple-element.139), channel_id=1, source_target_pairs={{4,0},{8,4},{12,8},{16,12},{20,16},{24,20},{28,24},{32,28},{36,32}... | collective-permute-start | bytes 196616 | tf_op jit(solution)/shard_map/ppermute | solution.py:23
  194.7 16.0 %collective-permute-start.31 = (f32[4,6,1,128]{3,2,1,0:T(1,128)S(1)}, f32[4,6,1,128]{3,2,1,0:T(1,128)S(1)}, u32[]{:S(2)}, u32[]{:S(2)}) collective-permute-start(f32[4,6,1,128]{3,2,1,0:T(1,128)S(1)} %get-tuple-element.109), channel_id=1, source_target_pairs={{1,0},{2,1},{3,2},{5,4},{6,5},{7,6},{9,8},{10,9},{11,10},{13,12},{... | collective-permute-start | bytes 36872 | tf_op jit(solution)/shard_map/ppermute | solution.py:23
  196.6 14.0 %collective-permute-start.30 = (f32[4,6,1,128]{3,2,1,0:T(1,128)S(1)}, f32[4,6,1,128]{3,2,1,0:T(1,128)S(1)}, u32[]{:S(2)}, u32[]{:S(2)}) collective-permute-start(f32[4,6,1,128]{3,2,1,0:T(1,128)S(1)} %get-tuple-element.108), channel_id=1, source_target_pairs={{0,1},{1,2},{2,3},{4,5},{5,6},{6,7},{8,9},{9,10},{10,11},{12,13},{... | collective-permute-start | bytes 36872 | tf_op jit(solution)/shard_map/ppermute | solution.py:20
  202.7 53.4 %collective-permute-start.35 = (f32[4,6,1,128]{3,2,1,0:T(1,128)S(1)}, f32[4,6,1,128]{3,2,1,0:T(1,128)S(1)}, u32[]{:S(2)}, u32[]{:S(2)}) collective-permute-start(f32[4,6,1,128]{3,2,1,0:T(1,128)S(1)} %get-tuple-element.107), channel_id=1, source_target_pairs={{1,0},{2,1},{3,2},{5,4},{6,5},{7,6},{9,8},{10,9},{11,10},{13,12},{... | collective-permute-start | bytes 36872 | tf_op jit(solution)/shard_map/ppermute | solution.py:23
  204.6 51.5 %collective-permute-start.34 = (f32[4,6,1,128]{3,2,1,0:T(1,128)S(1)}, f32[4,6,1,128]{3,2,1,0:T(1,128)S(1)}, u32[]{:S(2)}, u32[]{:S(2)}) collective-permute-start(f32[4,6,1,128]{3,2,1,0:T(1,128)S(1)} %get-tuple-element.106), channel_id=1, source_target_pairs={{0,1},{1,2},{2,3},{4,5},{5,6},{6,7},{8,9},{9,10},{10,11},{12,13},{... | collective-permute-start | bytes 36872 | tf_op jit(solution)/shard_map/ppermute | solution.py:20
  262.5 8.0 %collective-permute-start.39 = (f32[4,6,1,128]{3,2,1,0:T(1,128)S(1)}, f32[4,6,1,128]{3,2,1,0:T(1,128)S(1)}, u32[]{:S(2)}, u32[]{:S(2)}) collective-permute-start(f32[4,6,1,128]{3,2,1,0:T(1,128)S(1)} %get-tuple-element.105), channel_id=1, source_target_pairs={{1,0},{2,1},{3,2},{5,4},{6,5},{7,6},{9,8},{10,9},{11,10},{13,12},{... | collective-permute-start | bytes 36872 | tf_op jit(solution)/shard_map/ppermute | solution.py:23
  279.0 8.0 %collective-permute-start.43 = (f32[4,6,1,128]{3,2,1,0:T(1,128)S(1)}, f32[4,6,1,128]{3,2,1,0:T(1,128)S(1)}, u32[]{:S(2)}, u32[]{:S(2)}) collective-permute-start(f32[4,6,1,128]{3,2,1,0:T(1,128)S(1)} %get-tuple-element.103), channel_id=1, source_target_pairs={{1,0},{2,1},{3,2},{5,4},{6,5},{7,6},{9,8},{10,9},{11,10},{13,12},{... | collective-permute-start | bytes 36872 | tf_op jit(solution)/shard_map/ppermute | solution.py:23
  281.0 7.4 %collective-permute-start.42 = (f32[4,6,1,128]{3,2,1,0:T(1,128)S(1)}, f32[4,6,1,128]{3,2,1,0:T(1,128)S(1)}, u32[]{:S(2)}, u32[]{:S(2)}) collective-permute-start(f32[4,6,1,128]{3,2,1,0:T(1,128)S(1)} %get-tuple-element.102), channel_id=1, source_target_pairs={{0,1},{1,2},{2,3},{4,5},{5,6},{6,7},{8,9},{9,10},{10,11},{12,13},{... | collective-permute-start | bytes 36872 | tf_op jit(solution)/shard_map/ppermute | solution.py:20
  288.7 7.1 %collective-permute-start.45 = (f32[4,1,32,128]{3,2,1,0:T(8,128)S(1)}, f32[4,1,32,128]{3,2,1,0:T(8,128)S(1)}, u32[]{:S(2)}, u32[]{:S(2)}) collective-permute-start(f32[4,1,32,128]{3,2,1,0:T(8,128)S(1)} %get-tuple-element.131), channel_id=1, source_target_pairs={{4,0},{8,4},{12,8},{16,12},{20,16},{24,20},{28,24},{32,28},{36,32}... | collective-permute-start | bytes 196616 | tf_op jit(solution)/shard_map/ppermute | solution.py:23
  296.5 8.0 %collective-permute-start.47 = (f32[4,6,1,128]{3,2,1,0:T(1,128)S(1)}, f32[4,6,1,128]{3,2,1,0:T(1,128)S(1)}, u32[]{:S(2)}, u32[]{:S(2)}) collective-permute-start(f32[4,6,1,128]{3,2,1,0:T(1,128)S(1)} %get-tuple-element.101), channel_id=1, source_target_pairs={{1,0},{2,1},{3,2},{5,4},{6,5},{7,6},{9,8},{10,9},{11,10},{13,12},{... | collective-permute-start | bytes 36872 | tf_op jit(solution)/shard_map/ppermute | solution.py:23
  298.5 7.4 %collective-permute-start.46 = (f32[4,6,1,128]{3,2,1,0:T(1,128)S(1)}, f32[4,6,1,128]{3,2,1,0:T(1,128)S(1)}, u32[]{:S(2)}, u32[]{:S(2)}) collective-permute-start(f32[4,6,1,128]{3,2,1,0:T(1,128)S(1)} %get-tuple-element.100), channel_id=1, source_target_pairs={{0,1},{1,2},{2,3},{4,5},{5,6},{6,7},{8,9},{9,10},{10,11},{12,13},{... | collective-permute-start | bytes 36872 | tf_op jit(solution)/shard_map/ppermute | solution.py:20
  306.2 7.2 %collective-permute-start.49 = (f32[4,1,32,128]{3,2,1,0:T(8,128)S(1)}, f32[4,1,32,128]{3,2,1,0:T(8,128)S(1)}, u32[]{:S(2)}, u32[]{:S(2)}) collective-permute-start(f32[4,1,32,128]{3,2,1,0:T(8,128)S(1)} %get-tuple-element.129), channel_id=1, source_target_pairs={{4,0},{8,4},{12,8},{16,12},{20,16},{24,20},{28,24},{32,28},{36,32}... | collective-permute-start | bytes 196616 | tf_op jit(solution)/shard_map/ppermute | solution.py:23
  314.3 8.0 %collective-permute-start.51 = (f32[4,6,1,128]{3,2,1,0:T(1,128)S(1)}, f32[4,6,1,128]{3,2,1,0:T(1,128)S(1)}, u32[]{:S(2)}, u32[]{:S(2)}) collective-permute-start(f32[4,6,1,128]{3,2,1,0:T(1,128)S(1)} %get-tuple-element.99), channel_id=1, source_target_pairs={{1,0},{2,1},{3,2},{5,4},{6,5},{7,6},{9,8},{10,9},{11,10},{13,12},{... | collective-permute-start | bytes 36872 | tf_op jit(solution)/shard_map/ppermute | solution.py:23
  316.2 7.4 %collective-permute-start.50 = (f32[4,6,1,128]{3,2,1,0:T(1,128)S(1)}, f32[4,6,1,128]{3,2,1,0:T(1,128)S(1)}, u32[]{:S(2)}, u32[]{:S(2)}) collective-permute-start(f32[4,6,1,128]{3,2,1,0:T(1,128)S(1)} %get-tuple-element.98), channel_id=1, source_target_pairs={{0,1},{1,2},{2,3},{4,5},{5,6},{6,7},{8,9},{9,10},{10,11},{12,13},{... | collective-permute-start | bytes 36872 | tf_op jit(solution)/shard_map/ppermute | solution.py:20
  324.0 6.9 %collective-permute-start.53 = (f32[4,1,32,128]{3,2,1,0:T(8,128)S(1)}, f32[4,1,32,128]{3,2,1,0:T(8,128)S(1)}, u32[]{:S(2)}, u32[]{:S(2)}) collective-permute-start(f32[4,1,32,128]{3,2,1,0:T(8,128)S(1)} %get-tuple-element.127), channel_id=1, source_target_pairs={{4,0},{8,4},{12,8},{16,12},{20,16},{24,20},{28,24},{32,28},{36,32}... | collective-permute-start | bytes 196616 | tf_op jit(solution)/shard_map/ppermute | solution.py:23
  331.8 8.0 %collective-permute-start.55 = (f32[4,6,1,128]{3,2,1,0:T(1,128)S(1)}, f32[4,6,1,128]{3,2,1,0:T(1,128)S(1)}, u32[]{:S(2)}, u32[]{:S(2)}) collective-permute-start(f32[4,6,1,128]{3,2,1,0:T(1,128)S(1)} %get-tuple-element.97), channel_id=1, source_target_pairs={{1,0},{2,1},{3,2},{5,4},{6,5},{7,6},{9,8},{10,9},{11,10},{13,12},{... | collective-permute-start | bytes 36872 | tf_op jit(solution)/shard_map/ppermute | solution.py:23
  333.7 7.4 %collective-permute-start.54 = (f32[4,6,1,128]{3,2,1,0:T(1,128)S(1)}, f32[4,6,1,128]{3,2,1,0:T(1,128)S(1)}, u32[]{:S(2)}, u32[]{:S(2)}) collective-permute-start(f32[4,6,1,128]{3,2,1,0:T(1,128)S(1)} %get-tuple-element.96), channel_id=1, source_target_pairs={{0,1},{1,2},{2,3},{4,5},{5,6},{6,7},{8,9},{9,10},{10,11},{12,13},{... | collective-permute-start | bytes 36872 | tf_op jit(solution)/shard_map/ppermute | solution.py:20
  341.4 6.9 %collective-permute-start.57 = (f32[4,1,32,128]{3,2,1,0:T(8,128)S(1)}, f32[4,1,32,128]{3,2,1,0:T(8,128)S(1)}, u32[]{:S(2)}, u32[]{:S(2)}) collective-permute-start(f32[4,1,32,128]{3,2,1,0:T(8,128)S(1)} %get-tuple-element.125), channel_id=1, source_target_pairs={{4,0},{8,4},{12,8},{16,12},{20,16},{24,20},{28,24},{32,28},{36,32}... | collective-permute-start | bytes 196616 | tf_op jit(solution)/shard_map/ppermute | solution.py:23
  349.2 8.0 %collective-permute-start.59 = (f32[4,6,1,128]{3,2,1,0:T(1,128)S(1)}, f32[4,6,1,128]{3,2,1,0:T(1,128)S(1)}, u32[]{:S(2)}, u32[]{:S(2)}) collective-permute-start(f32[4,6,1,128]{3,2,1,0:T(1,128)S(1)} %get-tuple-element.95), channel_id=1, source_target_pairs={{1,0},{2,1},{3,2},{5,4},{6,5},{7,6},{9,8},{10,9},{11,10},{13,12},{... | collective-permute-start | bytes 36872 | tf_op jit(solution)/shard_map/ppermute | solution.py:23
  351.2 7.4 %collective-permute-start.58 = (f32[4,6,1,128]{3,2,1,0:T(1,128)S(1)}, f32[4,6,1,128]{3,2,1,0:T(1,128)S(1)}, u32[]{:S(2)}, u32[]{:S(2)}) collective-permute-start(f32[4,6,1,128]{3,2,1,0:T(1,128)S(1)} %get-tuple-element.94), channel_id=1, source_target_pairs={{0,1},{1,2},{2,3},{4,5},{5,6},{6,7},{8,9},{9,10},{10,11},{12,13},{... | collective-permute-start | bytes 36872 | tf_op jit(solution)/shard_map/ppermute | solution.py:20
  359.1 7.1 %collective-permute-start.61 = (f32[8,1,32,128]{3,2,1,0:T(8,128)S(1)}, f32[8,1,32,128]{3,2,1,0:T(8,128)S(1)}, u32[]{:S(2)}, u32[]{:S(2)}) collective-permute-start(f32[8,1,32,128]{3,2,1,0:T(8,128)S(1)} %get-tuple-element.91), channel_id=1, source_target_pairs={{4,0},{8,4},{12,8},{16,12},{20,16},{24,20},{28,24},{32,28},{36,32}... | collective-permute-start | bytes 393224 | tf_op jit(solution)/shard_map/ppermute | solution.py:23
  367.1 8.8 %collective-permute-start.63 = (f32[8,6,1,128]{3,2,1,0:T(1,128)S(1)}, f32[8,6,1,128]{3,2,1,0:T(1,128)S(1)}, u32[]{:S(2)}, u32[]{:S(2)}) collective-permute-start(f32[8,6,1,128]{3,2,1,0:T(1,128)S(1)} %get-tuple-element.83), channel_id=1, source_target_pairs={{1,0},{2,1},{3,2},{5,4},{6,5},{7,6},{9,8},{10,9},{11,10},{13,12},{... | collective-permute-start | bytes 73736 | tf_op jit(solution)/shard_map/ppermute | solution.py:23
  369.2 7.5 %collective-permute-start.62 = (f32[8,6,1,128]{3,2,1,0:T(1,128)S(1)}, f32[8,6,1,128]{3,2,1,0:T(1,128)S(1)}, u32[]{:S(2)}, u32[]{:S(2)}) collective-permute-start(f32[8,6,1,128]{3,2,1,0:T(1,128)S(1)} %get-tuple-element.82), channel_id=1, source_target_pairs={{0,1},{1,2},{2,3},{4,5},{5,6},{6,7},{8,9},{9,10},{10,11},{12,13},{... | collective-permute-start | bytes 73736 | tf_op jit(solution)/shard_map/ppermute | solution.py:20
  (38 other events, 501.0 us)
Sparse Core Ops, SparseCore 0:
  377.9 99.7 all-reduce.20
